TPU v7x, 256 devices: a whole 4x4x8 slice. The times are simulated.
256 devices in a mesh: frame: 16 (over z_lo, y, core), mp: 16 (over z_hi, x).
Axes of the slice: x: 4, y: 4, z: 8 (z_hi: 4, z_lo: 2; z = z_hi * 2 + z_lo), core: 2. Of those that a mesh axis runs over, the one named last changes fastest.
Arguments:
- tokens: bfloat16 [128, 2, 32, 3072], P('mp', None, 'frame'), may hold values from -6 to 6
- cotangent: bfloat16 [128, 2, 32, 3072], P('mp', None, 'frame'), may hold values from -8 to 8
- mod_shift: float32 [2, 32, 3072], P(None, 'frame'), may hold values from -3 to 3
- mod_scale: float32 [2, 32, 3072], P(None, 'frame'), may hold values from -0.5 to 5
- mod_gate: float32 [2, 32, 3072], P(None, 'frame'), may hold values from -4 to 4
- attn_weights: bfloat16 [3072, 4, 4096], P(None, None, 'mp'), may hold values from -1 to 1
Outputs:
- mixed: bfloat16 [128, 2, 32, 3072], P('mp', None, 'frame')
- grad_tokens: bfloat16 [128, 2, 32, 3072], P('mp', None, 'frame')
- weight_grads: float32 [3072, 4, 4096], P('frame', None, 'mp')
All inputs are finite; a program needn't handle non-finite values.
Results may differ from a plain program's by a relative error of at most 0.023.
Values may be sent and summed in bfloat16 or wider, within the bound.
A program may use at most 128 MiB of HBM per device.

v0:
```python
import jax
import jax.numpy as jnp
from jax import lax
from jax.sharding import PartitionSpec as P

HD = 128


EPSILON = 1e-06


def modulate(token_row_block, mod_shift, mod_scale):
    values = token_row_block.astype(jnp.float32)
    inverse_rms = lax.rsqrt(jnp.mean(values * values, axis=-1, keepdims=True) + EPSILON)
    unit_rows = values * inverse_rms
    normalized_rows = (unit_rows * (1.0 + mod_scale) + mod_shift).astype(jnp.bfloat16)
    return (normalized_rows, unit_rows, inverse_rms)


def split_heads(values):
    return values.reshape(values.shape[:3] + (values.shape[3] // HD, HD))


def merge_heads(values):
    return values.reshape(values.shape[:3] + (values.shape[3] * values.shape[4],))


def softmax_of(query_patch, key_patch, factor):
    scores = (
        jnp.einsum("pbfne,pbgne->pbnfg", query_patch, key_patch, preferred_element_type=jnp.float32)
        * factor
    )
    return jax.nn.softmax(scores, axis=-1)


def on_device(tokens, cotangent, mod_shift, mod_scale, mod_gate, attn_weights):
    model_width = tokens.shape[3]
    local_inner = attn_weights.shape[2]
    factor = HD ** (-0.5)
    weight_inputs = attn_weights[:, :3, :]
    w_out = attn_weights[:, 3, :]
    normalized_rows, unit_rows, inverse_rms = modulate(
        lax.all_gather(tokens, "mp", axis=0, tiled=True), mod_shift, mod_scale
    )
    projected = jnp.einsum(
        "tmwq,qcv->tmwcv", normalized_rows, weight_inputs, preferred_element_type=jnp.float32
    ).astype(jnp.bfloat16)
    projected = projected.reshape(projected.shape[:3] + (3 * local_inner,))
    gathered = jnp.concatenate([normalized_rows, projected], axis=3)
    query = gathered[..., model_width : model_width + local_inner]
    key_rows = gathered[..., model_width + local_inner : model_width + 2 * local_inner]
    value_rows = gathered[..., model_width + 2 * local_inner : model_width + 3 * local_inner]
    query_patch = lax.all_to_all(query, "frame", split_axis=0, concat_axis=2, tiled=True)
    key_patch = lax.all_to_all(key_rows, "frame", split_axis=0, concat_axis=2, tiled=True)
    value_patch = lax.all_to_all(value_rows, "frame", split_axis=0, concat_axis=2, tiled=True)
    attention = softmax_of(split_heads(query_patch), split_heads(key_patch), factor)
    attended_heads = jnp.einsum(
        "pbnfg,pbgne->pbfne",
        attention.astype(jnp.bfloat16),
        split_heads(value_patch),
        preferred_element_type=jnp.float32,
    ).astype(jnp.bfloat16)
    attended_back = lax.all_to_all(
        merge_heads(attended_heads), "frame", split_axis=2, concat_axis=0, tiled=True
    )
    attended, query_patch, key_patch, value_patch = (
        attended_back,
        query_patch,
        key_patch,
        value_patch,
    )
    scaled = (
        lax.all_gather(cotangent, "mp", axis=0, tiled=True).astype(jnp.float32) * mod_gate
    ).astype(jnp.bfloat16)
    backward = jnp.einsum(
        "pbfd,de->pbfe", scaled, w_out, preferred_element_type=jnp.float32
    ).astype(jnp.bfloat16)
    cot_gathered = jnp.concatenate([scaled, backward], axis=3)
    scaled_all = cot_gathered[..., :model_width]
    grad_attended = cot_gathered[..., model_width:]
    grad_patch = split_heads(
        lax.all_to_all(grad_attended, "frame", split_axis=0, concat_axis=2, tiled=True)
    )
    query_heads = split_heads(query_patch)
    key_heads = split_heads(key_patch)
    value_heads = split_heads(value_patch)
    attention = softmax_of(query_heads, key_heads, factor)
    attention_low = attention.astype(jnp.bfloat16)
    grad_value = jnp.einsum(
        "pbnfg,pbfne->pbgne", attention_low, grad_patch, preferred_element_type=jnp.float32
    ).astype(jnp.bfloat16)
    grad_probs = jnp.einsum(
        "pbfne,pbgne->pbnfg", grad_patch, value_heads, preferred_element_type=jnp.float32
    )
    grad_scores = (
        attention * (grad_probs - jnp.sum(grad_probs * attention, axis=-1, keepdims=True)) * factor
    ).astype(jnp.bfloat16)
    grad_query = jnp.einsum(
        "pbnfg,pbgne->pbfne", grad_scores, key_heads, preferred_element_type=jnp.float32
    ).astype(jnp.bfloat16)
    grad_key = jnp.einsum(
        "pbnfg,pbfne->pbgne", grad_scores, query_heads, preferred_element_type=jnp.float32
    ).astype(jnp.bfloat16)
    frame_query, frame_key, frame_value = (
        lax.all_to_all(merge_heads(grad_query), "frame", split_axis=2, concat_axis=0, tiled=True),
        lax.all_to_all(merge_heads(grad_key), "frame", split_axis=2, concat_axis=0, tiled=True),
        lax.all_to_all(merge_heads(grad_value), "frame", split_axis=2, concat_axis=0, tiled=True),
    )
    stacked_rows = jnp.stack([frame_query, frame_key, frame_value], axis=3)
    token_row_block = attended
    branch = lax.psum_scatter(
        jnp.einsum(
            "pbfe,de->pbfd", token_row_block, w_out, preferred_element_type=jnp.float32
        ).astype(jnp.bfloat16),
        "mp",
        scatter_dimension=0,
        tiled=True,
    ).astype(jnp.float32)
    token_row_block = stacked_rows
    grad_normed = lax.psum_scatter(
        jnp.einsum(
            "gxinc,qnc->gxiq", token_row_block, weight_inputs, preferred_element_type=jnp.float32
        ).astype(jnp.bfloat16),
        "mp",
        scatter_dimension=0,
        tiled=True,
    ).astype(jnp.float32)
    mixed = (tokens.astype(jnp.float32) + mod_gate * branch).astype(jnp.bfloat16)
    local_normed, unit_rows, inverse_rms = modulate(tokens, mod_shift, mod_scale)
    grad_unit = grad_normed * (1.0 + mod_scale)
    correction = jnp.mean(grad_unit * unit_rows, axis=-1, keepdims=True)
    grad_tokens = (
        cotangent.astype(jnp.float32) + inverse_rms * (grad_unit - unit_rows * correction)
    ).astype(jnp.bfloat16)
    normalized_full = gathered[..., :model_width]
    out_grads = jnp.einsum(
        "pbfd,pbfe->de", scaled_all, attended, preferred_element_type=jnp.float32
    )
    weight_grads = lax.psum_scatter(
        jnp.concatenate(
            [
                jnp.einsum(
                    "clrn,clrxt->nxt",
                    normalized_full,
                    stacked_rows,
                    preferred_element_type=jnp.float32,
                ),
                out_grads[:, None, :],
            ],
            axis=1,
        ).astype(jnp.bfloat16),
        "frame",
        scatter_dimension=0,
        tiled=True,
    ).astype(jnp.float32)
    return (mixed, grad_tokens, weight_grads)


def solution(mesh):
    placed = (
        P("mp", None, "frame", None),
        P("mp", None, "frame", None),
        P(None, "frame", None),
        P(None, "frame", None),
        P(None, "frame", None),
        P(None, None, "mp"),
    )
    return jax.shard_map(
        on_device,
        mesh=mesh,
        in_specs=placed,
        out_specs=(
            P("mp", None, "frame", None),
            P("mp", None, "frame", None),
            P("frame", None, "mp"),
        ),
        check_vma=False,
    )
```

profile of v0, /device:TPU:1, one launch (start us, length us, event | category | flops | bytes accessed | tf_op | source)
XLA Modules:
  0.0 487.3 jit_solution(12302458403158344677)
XLA Ops:
  7.2 0.7 all-gather.3.cloned.1.call-update
  8.0 0.7 all-gather.5.cloned.1.call-update
  8.7 0.8 broadcast_add_fusion
  9.5 72.4 %all-gather.3.cloned.1.call-done = bf16[128,2,2,3072]{3,2,1,0:T(2,128)(2,1)} async-done(((bf16[8,2,2,3072]{3,2,1,0:T(2,128)(2,1)}), bf16[128,2,2,3072]{3,2,1,0:T(2,128)(2,1)}) %all-gather.3.cloned.1.call-update) | async-done | bytes 3145744 | tf_op jit(solution)/shard_map/all_gather | solution.py:43
  81.9 3.0 fusion.2
  85.0 6.7 %fusion.11 = bf16[128,2,2,3,256]{4,0,3,2,1:T(8,128)(2,1)S(1)} fusion(bf16[3072,3,256]{2,1,0:T(4,128)(2,1)} %bitcast.128, f32[2,2,3072]{2,1,0:T(2,128)S(1)} %copy-done.17, f32[2,2,3072]{2,1,0:T(2,128)S(1)} %broadcast_add_fusion, f32[128,2,2]{0,2,1:T(2,128)S(1)} %add_rsqrt_fusion.1, bf16[128,2,2,3072]{3,2,1,0:T(2,128)(2,1)S(1)} %copy-done.3), kind=kOutput, calls=%fused_computation.21 | convolution fusion | flops 2424176640 | bytes 8751104 | tf_op jit(solution)/shard_map/tmwq,qcv->tmwcv/dot_general | solution.py:45
  91.7 0.4 copy.157
  92.1 0.8 fusion.87
  92.8 0.9 copy.161
  93.7 5.0 %all-to-all-start.1 = ((bf16[128,2,2,256]{3,2,1,0:T(2,128)(2,1)}), bf16[128,2,2,256]{3,2,1,0:T(2,128)(2,1)S(1)}, u32[]{:S(2)}, u32[]{:S(2)}) async-start(bf16[128,2,2,256]{3,2,1,0:T(2,128)(2,1)} %copy.161), calls=%async_computation.1 | async-start | bytes 524288 | tf_op jit(solution)/shard_map/all_to_all | solution.py:53
  98.7 0.9 copy.164
  99.6 7.4 %all-to-all-done.1 = bf16[128,2,2,256]{3,2,1,0:T(2,128)(2,1)S(1)} async-done(((bf16[128,2,2,256]{3,2,1,0:T(2,128)(2,1)}), bf16[128,2,2,256]{3,2,1,0:T(2,128)(2,1)S(1)}, u32[]{:S(2)}, u32[]{:S(2)}) %all-to-all-start.1) | async-done | bytes 262176 | tf_op jit(solution)/shard_map/all_to_all | solution.py:53
  107.0 5.3 %all-to-all-start.2 = ((bf16[128,2,2,256]{3,2,1,0:T(2,128)(2,1)}), bf16[128,2,2,256]{3,2,1,0:T(2,128)(2,1)}, u32[]{:S(2)}, u32[]{:S(2)}) async-start(bf16[128,2,2,256]{3,2,1,0:T(2,128)(2,1)} %copy.164), calls=%async_computation.2 | async-start | bytes 524288 | tf_op jit(solution)/shard_map/all_to_all | solution.py:54
  112.4 6.1 %slice.19 = bf16[3072,1,256]{2,1,0:T(2,128)(2,1)S(1)} slice(bf16[3072,4,256]{2,1,0:T(4,128)(2,1)} %param.11), slice={[0:3072], [3:4], [0:256]} | slice | bytes 3145728 | tf_op jit(solution)/shard_map/slice | solution.py:41
  118.5 32.1 %all-gather.5.cloned.1.call-done = bf16[128,2,2,3072]{3,2,1,0:T(2,128)(2,1)} async-done(((bf16[8,2,2,3072]{3,2,1,0:T(2,128)(2,1)}), bf16[128,2,2,3072]{3,2,1,0:T(2,128)(2,1)}) %all-gather.5.cloned.1.call-update) | async-done | bytes 3145744 | tf_op jit(solution)/shard_map/all_gather | solution.py:73
  150.6 3.9 fusion.20
  154.5 1.0 copy.178
  155.4 5.0 %all-to-all-start.4 = ((bf16[128,2,2,256]{3,2,1,0:T(2,128)(2,1)}), bf16[128,2,2,256]{3,2,1,0:T(2,128)(2,1)S(1)}, u32[]{:S(2)}, u32[]{:S(2)}) async-start(bf16[128,2,2,256]{3,2,1,0:T(2,128)(2,1)} %copy.178), calls=%async_computation.4 | async-start | bytes 524288 | tf_op jit(solution)/shard_map/all_to_all | solution.py:82
  160.5 1.8 copy.158
  162.3 5.3 %all-to-all-done.4 = bf16[128,2,2,256]{3,2,1,0:T(2,128)(2,1)S(1)} async-done(((bf16[128,2,2,256]{3,2,1,0:T(2,128)(2,1)}), bf16[128,2,2,256]{3,2,1,0:T(2,128)(2,1)S(1)}, u32[]{:S(2)}, u32[]{:S(2)}) %all-to-all-start.4) | async-done | bytes 262176 | tf_op jit(solution)/shard_map/all_to_all | solution.py:82
  167.6 4.3 all-to-all-start
  172.1 1.1 copy.315
  173.4 0.4 fusion.88
  173.7 0.4 fusion.24
  174.2 0.2 copy.218
  174.4 0.9 reshape.88
  175.2 3.9 all-to-all-done
  179.2 4.3 all-to-all-start.7
  183.6 0.3 fusion.43
  183.9 0.4 fusion.22
  184.3 0.2 copy.216
  184.5 0.9 reshape.86
  185.4 5.4 %all-to-all-done.7 = bf16[8,2,32,256]{3,1,0,2:T(2,128)(2,1)S(1)} async-done(((bf16[8,2,32,256]{3,1,0,2:T(2,128)(2,1)}), bf16[8,2,32,256]{3,1,0,2:T(2,128)(2,1)S(1)}, u32[]{:S(2)}, u32[]{:S(2)}) %all-to-all-start.7) | async-done | bytes 262176 | tf_op jit(solution)/shard_map/all_to_all | solution.py:107
  190.7 4.3 all-to-all-start.5
  195.1 0.3 fusion.23
  195.4 0.2 copy.217
  195.6 0.9 reshape.87
  196.5 5.8 %all-to-all-done.5 = bf16[8,2,32,256]{3,1,0,2:T(2,128)(2,1)S(1)} async-done(((bf16[8,2,32,256]{3,1,0,2:T(2,128)(2,1)}), bf16[8,2,32,256]{3,1,0,2:T(2,128)(2,1)S(1)}, u32[]{:S(2)}, u32[]{:S(2)}) %all-to-all-start.5) | async-done | bytes 262176 | tf_op jit(solution)/shard_map/all_to_all | solution.py:105
  202.3 4.3 all-to-all-start.6
  206.7 7.1 %all-to-all-done.6 = bf16[8,2,32,256]{3,1,0,2:T(2,128)(2,1)S(1)} async-done(((bf16[8,2,32,256]{3,1,0,2:T(2,128)(2,1)}), bf16[8,2,32,256]{3,1,0,2:T(2,128)(2,1)S(1)}, u32[]{:S(2)}, u32[]{:S(2)}) %all-to-all-start.6) | async-done | bytes 262176 | tf_op jit(solution)/shard_map/all_to_all | solution.py:106
  214.0 0.7 copy-done.12
  214.8 5.7 %bitcast_convert_fusion.1 = bf16[128,2,2,3072]{3,0,2,1:T(8,128)(2,1)S(1)} fusion(bf16[3072,3,256]{2,1,0:T(4,128)(2,1)} %bitcast.129, bf16[128,2,2,1,256]{4,0,3,2,1:T(8,128)(2,1)S(1)} %get-tuple-element.25, bf16[128,2,2,1,256]{4,0,3,2,1:T(8,128)(2,1)S(1)} %get-tuple-element.26, bf16[128,2,2,1,256]{4,0,3,2,1:T(8,128)(2,1)S(1)} %bitcast.142), kind=kOutput, calls=%fused_computation.10 | convolution fusion | flops 2418278400 | bytes 8650752 | tf_op jit(solution)/shard_map/gxinc,qnc->gxiq/dot_general | solution.py:121
  220.4 3.2 copy.224
  223.7 3.6 reshape.91
  227.3 0.9 copy-done.6
  228.2 2.3 fusion.21
  230.5 1.2 copy.215
  231.6 0.9 reshape.85
  232.5 13.0 %all_to_all.123 = bf16[8,2,32,256]{3,1,0,2:T(2,128)(2,1)S(1)} all-to-all(bf16[8,2,32,256]{3,1,0,2:T(2,128)(2,1)} %reshape.85), channel_id=1, replica_groups=mesh['frame'=16,'mp'=16] {'frame'}, dimensions={2} | all-to-all | bytes 524288 | tf_op jit(solution)/shard_map/all_to_all | solution.py:63
  245.5 1.0 convolution_convert_fusion
  246.6 3.2 copy.222
  249.8 3.6 reshape.89
  253.6 3.5 fusion.7
  257.1 3.8 bitcast_convert_fusion
  260.9 3.2 pad_maximum_fusion
  264.1 0.9 copy-done.2
  265.2 50.0 %reduce-scatter.12.cloned.1.call-done = bf16[8,12288]{1,0:T(8,128)(2,1)} async-done(((bf16[128,12288]{1,0:T(8,128)(2,1)}), bf16[8,12288]{1,0:T(8,128)(2,1)}) %reduce-scatter.12.cloned.1.call-update) | async-done | bytes 196624
  315.3 1.1 fusion.31
  316.4 91.7 %reduce-scatter.10.cloned.1.call-done = bf16[8,12288]{1,0:T(8,128)(2,1)} async-done(((bf16[128,12288]{1,0:T(8,128)(2,1)}), bf16[8,12288]{1,0:T(8,128)(2,1)}) %reduce-scatter.10.cloned.1.call-update) | async-done | bytes 196624
  408.1 1.2 fusion.35
  409.3 0.9 copy.202
  410.2 0.9 copy.201
  411.1 67.5 %reduce-scatter.8.cloned.1.call-done = bf16[192,4,256]{2,0,1:T(8,128)(2,1)} async-done(((bf16[3072,4,256]{2,0,1:T(8,128)(2,1)}), bf16[192,4,256]{2,0,1:T(8,128)(2,1)}) %reduce-scatter.8.cloned.1.call-update) | async-done | bytes 393232 | tf_op jit(solution)/shard_map/reduce_scatter | solution.py:139
  478.6 2.2 copy.203
  (64 shorter events, 1.2 us)
Async XLA Ops:
  7.2 77.8 %copy-start.17 = (f32[2,2,3072]{2,1,0:T(2,128)S(1)}, f32[2,2,3072]{2,1,0:T(2,128)}, u32[]{:S(2)}) copy-start(f32[2,2,3072]{2,1,0:T(2,128)} %param.8) | copy-start | bytes 147460
  7.2 74.7 %all-gather.3.cloned.1.call-start = ((), (), s32[]{:S(2)}) async-start(), calls=%async_computation.11 | async-start | bytes 3342336 | tf_op jit(solution)/shard_map/all_gather | solution.py:43
  7.9 142.7 %all-gather.5.cloned.1.call-start = ((), (), s32[]{:S(2)}) async-start(), calls=%async_computation.12 | async-start | bytes 3342336 | tf_op jit(solution)/shard_map/all_gather | solution.py:73
  81.9 3.1 copy-start.3
  93.7 13.3 %all-to-all-start.1 = ((bf16[128,2,2,256]{3,2,1,0:T(2,128)(2,1)}), bf16[128,2,2,256]{3,2,1,0:T(2,128)(2,1)S(1)}, u32[]{:S(2)}, u32[]{:S(2)}) async-start(bf16[128,2,2,256]{3,2,1,0:T(2,128)(2,1)} %copy.161), calls=%async_computation.1 | async-start | bytes 524288 | tf_op jit(solution)/shard_map/all_to_all | solution.py:53
  107.0 48.4 %all-to-all-start.2 = ((bf16[128,2,2,256]{3,2,1,0:T(2,128)(2,1)}), bf16[128,2,2,256]{3,2,1,0:T(2,128)(2,1)}, u32[]{:S(2)}, u32[]{:S(2)}) async-start(bf16[128,2,2,256]{3,2,1,0:T(2,128)(2,1)} %copy.164), calls=%async_computation.2 | async-start | bytes 524288 | tf_op jit(solution)/shard_map/all_to_all | solution.py:54
  112.4 38.2 %copy-start.16 = (f32[2,2,3072]{2,1,0:T(2,128)S(1)}, f32[2,2,3072]{2,1,0:T(2,128)}, u32[]{:S(2)}) copy-start(f32[2,2,3072]{2,1,0:T(2,128)} %param.10) | copy-start | bytes 147460
  118.5 36.0 %copy-start = (bf16[3072,1,256]{2,1,0:T(2,128)(2,1)}, bf16[3072,1,256]{2,1,0:T(2,128)(2,1)S(1)}, u32[]{:S(2)}) copy-start(bf16[3072,1,256]{2,1,0:T(2,128)(2,1)S(1)} %slice.19) | copy-start | bytes 4718596
  155.4 12.2 %all-to-all-start.4 = ((bf16[128,2,2,256]{3,2,1,0:T(2,128)(2,1)}), bf16[128,2,2,256]{3,2,1,0:T(2,128)(2,1)S(1)}, u32[]{:S(2)}, u32[]{:S(2)}) async-start(bf16[128,2,2,256]{3,2,1,0:T(2,128)(2,1)} %copy.178), calls=%async_computation.4 | async-start | bytes 524288 | tf_op jit(solution)/shard_map/all_to_all | solution.py:82
  167.6 11.5 %all-to-all-start = ((bf16[128,2,2,256]{3,2,1,0:T(2,128)(2,1)}), bf16[128,2,2,256]{3,2,1,0:T(2,128)(2,1)S(1)}, u32[]{:S(2)}, u32[]{:S(2)}) async-start(bf16[128,2,2,256]{3,2,1,0:T(2,128)(2,1)} %copy.158), calls=%async_computation | async-start | bytes 524288 | tf_op jit(solution)/shard_map/all_to_all | solution.py:55
  172.1 23.0 %copy-start.8 = (bf16[8,2,32,2,128]{4,3,0,2,1:T(2,128)(2,1)}, bf16[8,2,32,2,128]{4,3,0,2,1:T(2,128)(2,1)S(1)}, u32[]{:S(2)}) copy-start(bf16[8,2,32,2,128]{4,3,0,2,1:T(2,128)(2,1)S(1)} %reshape.71) | copy-start | bytes 786436
  173.2 10.6 %copy-start.9 = (bf16[8,2,32,2,128]{4,3,0,2,1:T(2,128)(2,1)}, bf16[8,2,32,2,128]{4,3,0,2,1:T(2,128)(2,1)S(1)}, u32[]{:S(2)}) copy-start(bf16[8,2,32,2,128]{4,3,0,2,1:T(2,128)(2,1)S(1)} %reshape.72) | copy-start | bytes 786436
  179.2 11.6 %all-to-all-start.7 = ((bf16[8,2,32,256]{3,1,0,2:T(2,128)(2,1)}), bf16[8,2,32,256]{3,1,0,2:T(2,128)(2,1)S(1)}, u32[]{:S(2)}, u32[]{:S(2)}) async-start(bf16[8,2,32,256]{3,1,0,2:T(2,128)(2,1)} %reshape.88), calls=%async_computation.7 | async-start | bytes 524288 | tf_op jit(solution)/shard_map/all_to_all | solution.py:107
  183.6 11.4 %copy-start.5 = (bf16[8,2,32,2,128]{4,3,0,2,1:T(2,128)(2,1)}, bf16[8,2,32,2,128]{4,3,0,2,1:T(2,128)(2,1)S(1)}, u32[]{:S(2)}) copy-start(bf16[8,2,32,2,128]{4,3,0,2,1:T(2,128)(2,1)S(1)} %reshape.70) | copy-start | bytes 786436
  190.7 11.6 %all-to-all-start.5 = ((bf16[8,2,32,256]{3,1,0,2:T(2,128)(2,1)}), bf16[8,2,32,256]{3,1,0,2:T(2,128)(2,1)S(1)}, u32[]{:S(2)}, u32[]{:S(2)}) async-start(bf16[8,2,32,256]{3,1,0,2:T(2,128)(2,1)} %reshape.86), calls=%async_computation.5 | async-start | bytes 524288 | tf_op jit(solution)/shard_map/all_to_all | solution.py:105
  202.3 11.6 %all-to-all-start.6 = ((bf16[8,2,32,256]{3,1,0,2:T(2,128)(2,1)}), bf16[8,2,32,256]{3,1,0,2:T(2,128)(2,1)S(1)}, u32[]{:S(2)}, u32[]{:S(2)}) async-start(bf16[8,2,32,256]{3,1,0,2:T(2,128)(2,1)} %reshape.87), calls=%async_computation.6 | async-start | bytes 524288 | tf_op jit(solution)/shard_map/all_to_all | solution.py:106
  206.6 108.7 %reduce-scatter.12.cloned.1.call-start = ((), (), s32[]{:S(2)}) async-start(), calls=%async_computation.15 | async-start | bytes 3342336
  206.7 7.2 %copy-start.10 = (bf16[16,8,2,2,256]{4,1,0,3,2:T(8,128)(2,1)}, bf16[16,8,2,2,256]{4,1,0,3,2:T(8,128)(2,1)S(1)}, u32[]{:S(2)}) copy-start(bf16[16,8,2,2,256]{4,1,0,3,2:T(8,128)(2,1)S(1)} %copy.313) | copy-start | bytes 786436
  213.9 0.7 copy-start.12
  213.9 0.8 copy-start.14
  227.2 0.9 copy-start.6
  227.3 18.3 %copy-start.1 = (bf16[3072,1,256]{2,1,0:T(2,128)(2,1)S(1)}, bf16[3072,1,256]{2,1,0:T(2,128)(2,1)}, u32[]{:S(2)}) copy-start(bf16[3072,1,256]{2,1,0:T(2,128)(2,1)} %copy-done) | copy-start | bytes 4718596
  227.3 180.8 %reduce-scatter.10.cloned.1.call-start = ((), (), s32[]{:S(2)}) async-start(), calls=%async_computation.14 | async-start | bytes 3342336
  253.5 3.6 copy-start.4
  253.5 225.2 %reduce-scatter.8.cloned.1.call-start = ((), (), s32[]{:S(2)}) async-start(), calls=%async_computation.13 | async-start | bytes 6684672 | tf_op jit(solution)/shard_map/reduce_scatter | solution.py:139
  253.5 3.5 copy-start.11
  253.5 3.5 copy-start.13
  253.5 3.5 copy-start.15
  253.6 3.5 copy-start.18
  264.1 0.9 copy-start.2
  264.1 144.0 %copy-start.7 = (bf16[8,2,2,3072]{3,2,1,0:T(2,128)(2,1)S(1)}, bf16[8,2,2,3072]{3,2,1,0:T(2,128)(2,1)}, u32[]{:S(2)}) copy-start(bf16[8,2,2,3072]{3,2,1,0:T(2,128)(2,1)} %param.7) | copy-start | bytes 589828
Sparse Core Ops, SparseCore 0:
  10.4 71.3 all-gather.2
  84.3 66.2 all-gather.4
  227.4 87.8 reduce-scatter.11
  318.7 89.3 reduce-scatter.9
  410.5 68.0 reduce-scatter.7
where the time goes:
time: 491 us; the launch traced here: 487 us
  waiting for transfers between devices  350 us (71%)
  local copies, waits for them, and re-layouts  39 us (8%)
  starting transfers between devices  32.8 us (7%)
  matrix products  28.6 us (6%)
  between operations  14.2 us (3%)
  blocking collectives  13 us (3%)
  other arithmetic  9.63 us (2%)
    unnamed x7, waiting for transfers between devices  143 us
    all_gather x1, waiting for transfers between devices, on_device(): lax.all_gather(tokens, 'mp', axis=0, tiled=True)  72.4 us
    reduce_scatter x1, waiting for transfers between devices, on_device(): lax.psum_scatter(jnp.concatenate([jnp.einsum('clrn,clrxt->nxt', normalize...  67.5 us
    all_gather x1, waiting for transfers between devices, on_device(): lax.all_gather(cotangent, 'mp', axis=0, tiled=True).astype(jnp.float32)  32.1 us
    unnamed x45, local copies, waits for them, and re-layouts  20.3 us
    all_to_all x1, blocking collectives, on_device(): lax.all_to_all(merge_heads(attended_heads), 'frame', split_axis=2, concat...  13 us
  transfers between devices with their start and end apart: 12, of which 11 were waited for; matrix products, arithmetic and copies ran while one was open for 12% of the time, Pallas kernels for 0%

commit v1 on v0

v1 whole, which is shorter than its diff:
```python
import jax
import jax.numpy as jnp
from jax import lax
from jax.experimental import pallas as pl
from jax.experimental.pallas import tpu as pltpu
from jax.sharding import PartitionSpec as P

HD = 128
D = 3072
EPSILON = 1e-06
MESH = pl.DeviceIdType.MESH
BF16 = jnp.bfloat16
F32 = jnp.float32
MIB = 1024 * 1024


def dot(a, b, dims=((1,), (0,))):
    return lax.dot_general(a, b, (dims, ((), ())), preferred_element_type=F32)


NT = ((1,), (1,))
TN = ((0,), (0,))


class Ring:
    def __init__(self, index, device, stride):
        self.index, self.device, self.stride = index, device, stride

    def at(self, step):
        return lax.rem(self.index + (step + 4), 4)

    def to(self, step):
        return self.device(self.at(step))


class Links:
    def __init__(self, send_sems, recv_sems):
        self.send_sems, self.recv_sems = send_sems, recv_sems
        self.copies = []

    def copy(self, source, target, device):
        number = len(self.copies)
        made = pltpu.make_async_remote_copy(
            src_ref=source,
            dst_ref=target,
            send_sem=self.send_sems.at[number],
            recv_sem=self.recv_sems.at[number],
            device_id=device,
            device_id_type=MESH,
        )
        self.copies.append(made)
        return made

    def drain(self):
        for made in self.copies:
            made.wait_send()


def block_rows(first, second, one, two, half):
    block = first.at(one) * first.stride + second.at(two) * second.stride
    start = block * 32 + (0 if half is None else 16 * half)
    size = 32 if half is None else 16
    return pl.ds(pl.multiple_of(start, size), size)


def gather_events(links, buffer, columns, first, second):
    def message(ring, step, one, two, half=None):
        part = buffer.at[block_rows(first, second, one, two, half), columns]
        return links.copy(part, part, ring.to(step))

    ahead, back = message(first, 1, 0, 0), message(first, -1, 0, 0)
    ahead_far, back_far = message(first, 1, -1, 0, 0), message(first, -1, 1, 0, 1)
    near, far = {}, {}
    for one in (0, -1, 1, 2):
        near[one] = message(second, 1, one, 0), message(second, -1, one, 0)
        far[one] = message(second, 1, one, -1, 0), message(second, -1, one, 1, 1)

    def begin():
        for made in (ahead, back) + near[0]:
            made.start()

    def from_behind():
        ahead.wait_recv()
        for made in (ahead_far,) + near[-1]:
            made.start()

    def from_ahead():
        back.wait_recv()
        for made in (back_far,) + near[1]:
            made.start()

    def from_across():
        ahead_far.wait_recv()
        back_far.wait_recv()
        for made in near[2]:
            made.start()

    def onward(one):
        def event():
            for arrived, following in zip(near[one], far[one]):
                arrived.wait_recv()
                following.start()

        return event

    def end():
        for pair in far.values():
            for made in pair:
                made.wait_recv()

    return [begin, from_behind, from_ahead, onward(0), from_across, onward(-1), onward(1), onward(2), end]


def add_to(target, *others):
    total = target[...].astype(F32)
    for other in others:
        total = total + other[...].astype(F32)
    target[...] = total.astype(target.dtype)


class RingSum:
    def __init__(self, links, ring, piece, first, second):
        self.piece, self.first, self.second = piece, first, second
        ahead, back = ring.to(1), ring.to(-1)
        self.far = (
            links.copy(piece(2, 0), first(0), ahead),
            links.copy(piece(2, 1), first(1), back),
        )
        self.own = (
            links.copy(piece(1, 1), second(0, 1), ahead),
            links.copy(piece(-1, 0), second(1, 0), back),
        )
        self.summed = (
            links.copy(piece(1, 0), second(0, 0), ahead),
            links.copy(piece(-1, 1), second(1, 1), back),
        )

    def begin(self):
        for made in self.far + self.own:
            made.start()

    def onward(self):
        for side, target in enumerate((self.piece(1, 0), self.piece(-1, 1))):
            self.far[side].wait_recv()
            add_to(target, self.first(side))
            self.summed[side].start()

    def end(self):
        for made in self.own + self.summed:
            made.wait_recv()
        for half in range(2):
            add_to(self.piece(0, half), self.second(0, half), self.second(1, half))


def scatter_events(links, buffer, columns, first, second, land1, land2):
    def over_first(slot, two):
        return RingSum(
            links,
            first,
            lambda one, half: buffer.at[block_rows(first, second, one, two, half), columns],
            lambda side: land1.at[slot, side, :, columns],
            lambda side, half: land2.at[slot, side, 16 * half : 16 * half + 16, columns],
        )

    rows = [over_first(slot, two) for slot, two in enumerate((2, -1, 1, 0))]
    column = RingSum(
        links,
        second,
        lambda two, half: buffer.at[block_rows(first, second, 0, two, half), columns],
        lambda side: land1.at[4, side, :, columns],
        lambda side, half: land2.at[4, side, 16 * half : 16 * half + 16, columns],
    )

    def begin():
        for row in rows:
            row.begin()

    def onward(row):
        return row.onward

    def end_rows():
        for row in rows:
            row.end()

    return [begin] + [row.onward for row in rows] + [end_rows, column.begin, column.onward, column.end]


def softmax_rows(scores):
    shifted = jnp.exp(scores - jnp.max(scores, axis=-1, keepdims=True))
    return shifted / jnp.sum(shifted, axis=-1, keepdims=True)


def same_block():
    rows = lax.broadcasted_iota(jnp.int32, (HD, HD), 0)
    columns = lax.broadcasted_iota(jnp.int32, (HD, HD), 1)
    return (rows >> 5) == (columns >> 5)


def kernel(
    x0, w_hbm, out, dw,
    xall, w, qkv, grad_att, dall, turned, probs, branch, grad, dpart,
    land1b, land2b, land1g, land2g, land_core, land1y, land2y, land_z, flipped, core_out, core_in,
    send_sems, recv_sems, local_sems,
):
    f, m = lax.axis_index("frame"), lax.axis_index("mp")
    x, z = lax.rem(m, 4), lax.div(m, 4)
    core, y, zl = lax.rem(f, 2), lax.rem(lax.div(f, 2), 4), lax.div(f, 8)
    other = 1 - core
    ring_x = Ring(x, lambda to: (f, z * 4 + to), 1)
    ring_z = Ring(z, lambda to: (f, to * 4 + x), 4)
    ring_y = Ring(y, lambda to: (zl * 8 + to * 2 + core, m), 0)
    z_partner = ((1 - zl) * 8 + y * 2 + core, m)
    core_partner = (zl * 8 + y * 2 + other, m)
    links = Links(send_sems, recv_sems)

    own_rows = pl.ds(pl.multiple_of(m * 32, 32), 32)
    take = pltpu.make_async_copy(x0, xall.at[own_rows, :], local_sems.at[0])
    take.start()
    weigh = pltpu.make_async_copy(w_hbm, w, local_sems.at[1])
    weigh.start()
    barrier = pltpu.get_barrier_semaphore()
    for ring in (ring_x, ring_z, ring_y):
        for step in (1, -1):
            pl.semaphore_signal(barrier, inc=1, device_id=ring.to(step), device_id_type=MESH)
    for partner in (z_partner, core_partner):
        pl.semaphore_signal(barrier, inc=1, device_id=partner, device_id_type=MESH)
    pl.semaphore_wait(barrier, 8)
    take.wait()

    normed = gather_events(links, xall, slice(0, D), ring_z, ring_x)
    scaled = gather_events(links, xall, slice(D, 2 * D), ring_z, ring_x)
    sum_branch = scatter_events(links, branch, slice(0, D), ring_x, ring_z, land1b, land2b)
    sum_grad = scatter_events(links, grad, slice(0, D), ring_x, ring_z, land1g, land2g)

    def chip_columns(y_to, zl_to):
        return pl.ds(pl.multiple_of(zl_to * 1536 + y_to * 384, 128), 384)

    mine = pl.multiple_of(core * 512, 512)
    theirs = pl.multiple_of(other * 512, 512)
    chunks = [(step, side) for step in (2, 1, -1, 0) for side in (1, 0)]
    core_copies = {}
    for step, side in chunks:
        columns = chip_columns(ring_y.at(step), lax.rem(zl + side, 2))
        core_copies[step, side] = links.copy(
            dpart.at[pl.ds(theirs, 512), columns], land_core.at[:, columns], core_partner
        )

    def over_y(side):
        zl_to = lax.rem(zl + side, 2)
        return RingSum(
            links,
            ring_y,
            lambda step, half: dpart.at[
                pl.ds(pl.multiple_of(mine + 256 * half, 256), 256), chip_columns(ring_y.at(step), zl_to)
            ],
            lambda go: land1y.at[side, go],
            lambda go, half: land2y.at[side, go, 256 * half : 256 * half + 256],
        )

    y_sums = [over_y(0), over_y(1)]
    z_copy = links.copy(
        dpart.at[pl.ds(mine, 512), chip_columns(y, 1 - zl)], land_z, z_partner
    )
    core_copy = links.copy(core_out, core_in, core_partner)

    def project(slot):
        qkv[:, 256 * slot : 256 * slot + 256] = dot(
            xall[:, :D], w[:, 256 * slot : 256 * slot + 256]
        ).astype(BF16)

    def attend():
        mask = same_block()

        @pl.loop(0, 4)
        def _(group):
            rows = pl.ds(pl.multiple_of(group * HD, HD), HD)
            for head in range(2):
                query = qkv[rows, head * HD : head * HD + HD]
                key = qkv[rows, 256 + head * HD : 256 + head * HD + HD]
                value = qkv[rows, 512 + head * HD : 512 + head * HD + HD]
                scores = dot(query, key, NT) * (HD ** -0.5)
                attention = softmax_rows(jnp.where(mask, scores, -1e30))
                probs[group * 2 + head] = attention
                dall[rows, 768 + head * HD : 768 + head * HD + HD] = dot(
                    attention.astype(BF16), value
                ).astype(BF16)

    def branch_part(step):
        rows = pl.ds(pl.multiple_of(step * 512, 512), 512)
        branch[:, rows] = dot(dall[:, 768:], w[rows, 768:], NT).astype(BF16)

    def all_branch():
        pl.loop(0, 6)(branch_part)

    def back_project():
        grad_att[...] = dot(xall[:, D:], w[:, 768:]).astype(BF16)

    def attend_back():
        @pl.loop(0, 4)
        def _(group):
            rows = pl.ds(pl.multiple_of(group * HD, HD), HD)
            for head in range(2):
                low = slice(head * HD, head * HD + HD)
                query = qkv[rows, head * HD : head * HD + HD]
                key = qkv[rows, 256 + head * HD : 256 + head * HD + HD]
                value = qkv[rows, 512 + head * HD : 512 + head * HD + HD]
                incoming = grad_att[rows, low]
                attention = probs[group * 2 + head]
                grad_probs = dot(incoming, value, NT)
                inner = jnp.sum(grad_probs * attention, axis=-1, keepdims=True)
                grad_scores = (attention * (grad_probs - inner) * (HD ** -0.5)).astype(BF16)
                dall[rows, head * HD : head * HD + HD] = dot(grad_scores, key).astype(BF16)
                dall[rows, 256 + head * HD : 256 + head * HD + HD] = dot(
                    grad_scores, query, TN
                ).astype(BF16)
                dall[rows, 512 + head * HD : 512 + head * HD + HD] = dot(
                    attention.astype(BF16), incoming, TN
                ).astype(BF16)

    def grad_part(step):
        rows = pl.ds(pl.multiple_of(step * 512, 512), 512)
        grad[:, rows] = dot(dall[:, :768], w[rows, :768], NT).astype(BF16)

    def all_grad():
        pl.loop(0, 6)(grad_part)

    def turn():
        for part in range(8):
            turned[part * HD : part * HD + HD, :] = dall[:, part * HD : part * HD + HD].T

    def weight_chunk(step, side):
        def event():
            zl_to = lax.rem(zl + side, 2)
            columns = chip_columns(ring_y.at(step), zl_to)
            gated = pl.ds(pl.multiple_of(D + zl_to * 1536 + ring_y.at(step) * 384, 128), 384)
            dpart[:768, columns] = dot(turned[:768, :], xall[:, columns]).astype(BF16)
            dpart[768:, columns] = dot(turned[768:, :], xall[:, gated]).astype(BF16)
            core_copies[step, side].start()

        return event

    def core_sum(step, side):
        def event():
            columns = chip_columns(ring_y.at(step), lax.rem(zl + side, 2))
            core_copies[step, side].wait_recv()
            add_to(dpart.at[pl.ds(mine, 512), columns], land_core.at[:, columns])

        return event

    def z_end():
        z_copy.wait_recv()
        columns = chip_columns(y, zl)
        total = dpart[pl.ds(mine, 512), columns].astype(F32) + land_z[...].astype(F32)
        flipped[...] = total.T
        core_out[...] = flipped[pl.ds(pl.multiple_of(other * 192, 192), 192), :].astype(BF16)
        core_copy.start()
        dw[:, pl.ds(mine, 512)] = flipped[pl.ds(pl.multiple_of(core * 192, 192), 192), :]

    def core_end():
        core_copy.wait_recv()
        dw[:, pl.ds(theirs, 512)] = core_in[...].astype(F32)

    n, s, b, g = normed, scaled, sum_branch, sum_grad
    plan = [
        *n[:5], s[0], *n[5:8], s[1], s[2], n[8],
        weigh.wait,
        lambda: project(0), s[3], lambda: project(1), s[4], lambda: project(2), s[5],
        attend, s[6], all_branch, s[7],
        b[0],
        s[8],
        back_project, b[1], attend_back, b[2], all_grad, g[0], b[3], b[4],
        turn,
        *[weight_chunk(*chunk) for chunk in chunks[:4]],
        b[5], b[6],
        *[core_sum(*chunk) for chunk in chunks[:2]],
        *[weight_chunk(*chunk) for chunk in chunks[4:]],
        g[1], g[2],
        *[core_sum(*chunk) for chunk in chunks[2:6]],
        y_sums[1].begin, y_sums[0].begin,
        b[7], g[3], g[4],
        *[core_sum(*chunk) for chunk in chunks[6:]],
        b[8],
        y_sums[1].onward, y_sums[0].onward,
        g[5], g[6],
        y_sums[1].end, z_copy.start,
        g[7],
        y_sums[0].end,
        z_end,
        g[8],
        core_end,
    ]
    for event in plan:
        event()
    out[:, :D] = branch[own_rows, :]
    out[:, D:] = grad[own_rows, :]
    links.drain()


def exchange_and_compute(x0, weights):
    copies = 160
    return pl.pallas_call(
        kernel,
        out_shape=(
            jax.ShapeDtypeStruct((32, 2 * D), BF16),
            jax.ShapeDtypeStruct((192, 1024), F32),
        ),
        in_specs=[pl.BlockSpec(memory_space=pl.ANY)] * 2,
        out_specs=[pl.BlockSpec(memory_space=pltpu.VMEM)] * 2,
        scratch_shapes=[
            pltpu.VMEM((512, 2 * D), BF16),
            pltpu.VMEM((D, 1024), BF16),
            pltpu.VMEM((512, 768), BF16),
            pltpu.VMEM((512, 256), BF16),
            pltpu.VMEM((512, 1024), BF16),
            pltpu.VMEM((1024, 512), BF16),
            pltpu.VMEM((8, HD, HD), F32),
            pltpu.VMEM((512, D), BF16),
            pltpu.VMEM((512, D), BF16),
            pltpu.VMEM((1024, D), BF16),
            pltpu.VMEM((5, 2, 16, D), BF16),
            pltpu.VMEM((5, 2, 32, D), BF16),
            pltpu.VMEM((5, 2, 16, D), BF16),
            pltpu.VMEM((5, 2, 32, D), BF16),
            pltpu.VMEM((512, D), BF16),
            pltpu.VMEM((2, 2, 256, 384), BF16),
            pltpu.VMEM((2, 2, 512, 384), BF16),
            pltpu.VMEM((512, 384), BF16),
            pltpu.VMEM((384, 512), F32),
            pltpu.VMEM((192, 512), BF16),
            pltpu.VMEM((192, 512), BF16),
            pltpu.SemaphoreType.DMA((copies,)),
            pltpu.SemaphoreType.DMA((copies,)),
            pltpu.SemaphoreType.DMA((2,)),
        ],
        compiler_params=pltpu.CompilerParams(
            collective_id=0, has_side_effects=True, vmem_limit_bytes=60 * MIB
        ),
    )(x0, weights)


def on_device(tokens, cotangent, mod_shift, mod_scale, mod_gate, attn_weights):
    values = tokens.astype(F32)
    inverse_rms = lax.rsqrt(jnp.mean(values * values, axis=-1, keepdims=True) + EPSILON)
    unit = values * inverse_rms
    normed = (unit * (1.0 + mod_scale) + mod_shift).astype(BF16)
    scaled = (cotangent.astype(F32) * mod_gate).astype(BF16)
    rows = jnp.concatenate([normed, scaled], axis=-1).reshape(16, 2, 2 * D)
    rows = lax.all_to_all(rows, "frame", split_axis=0, concat_axis=0, tiled=True)
    sums, weight_grads = exchange_and_compute(
        rows.reshape(32, 2 * D), attn_weights.reshape(D, 1024)
    )
    sums = lax.all_to_all(
        sums.reshape(16, 2, 2 * D), "frame", split_axis=0, concat_axis=0, tiled=True
    ).reshape(8, 2, 2, 2 * D)
    branch, grad_normed = sums[..., :D].astype(F32), sums[..., D:].astype(F32)
    mixed = (values + mod_gate * branch).astype(BF16)
    grad_unit = grad_normed * (1.0 + mod_scale)
    correction = jnp.mean(grad_unit * unit, axis=-1, keepdims=True)
    grad_tokens = (
        cotangent.astype(F32) + inverse_rms * (grad_unit - unit * correction)
    ).astype(BF16)
    return mixed, grad_tokens, weight_grads.reshape(192, 4, 256)


def solution(mesh):
    placed = (
        P("mp", None, "frame", None),
        P("mp", None, "frame", None),
        P(None, "frame", None),
        P(None, "frame", None),
        P(None, "frame", None),
        P(None, None, "mp"),
    )
    return jax.shard_map(
        on_device,
        mesh=mesh,
        in_specs=placed,
        out_specs=(
            P("mp", None, "frame", None),
            P("mp", None, "frame", None),
            P("frame", None, "mp"),
        ),
        check_vma=False,
    )
```

time: 491 us -> 191 us (0.39)
  waiting for transfers between devices: 350 us -> 6.91 us
  Pallas kernels: 0 us -> 153 us
  matrix products: 28.6 us -> 0 us
  local copies, waits for them, and re-layouts: 39 us -> 12.8 us
  starting transfers between devices: 32.8 us -> 11 us
  between operations: 14.2 us -> 0.67 us
  blocking collectives: 13 us -> 0 us
    pallas_call x0 -> x1, Pallas kernels: none -> 153 us  [exchange_and_compute(): pl.pallas_call(kernel, out_shape=(jax.ShapeDtypeStruct((32, 2 * D), BF16)...]
    unnamed x7 -> x0, waiting for transfers between devices: 143 us -> none
    all_gather x2 -> x0, waiting for transfers between devices: 104 us -> none  [the longest x1 72.4 us: on_device(): lax.all_gather(tokens, 'mp', axis=0, tiled=True)]
    reduce_scatter x1 -> x0, waiting for transfers between devices: 67.5 us -> none  [on_device(): lax.psum_scatter(jnp.concatenate([jnp.einsum('clrn,clrxt->nxt', normalize...]
    dot_general x11 -> x0, matrix products: 28.2 us -> none  [the longest x1 6.74 us: on_device(): jnp.einsum('tmwq,qcv->tmwcv', normalized_rows, weight_inputs, preferred_e...]
    all_to_all x7 -> x2, waiting for transfers between devices: 35 us -> 6.91 us  [the longest x1 6.02 us: on_device(): lax.all_to_all(sums.reshape(16, 2, 2 * D), 'frame', split_axis=0, concat_...]
    all_to_all x7 -> x2, starting transfers between devices: 32.6 us -> 11 us  [the longest x1 7.34 us: on_device(): lax.all_to_all(rows, 'frame', split_axis=0, concat_axis=0, tiled=True)]
    all_to_all x1 -> x0, blocking collectives: 13 us -> none  [on_device(): lax.all_to_all(merge_heads(attended_heads), 'frame', split_axis=2, concat...]
  transfers between devices with their start and end apart: 12 -> 2, of which waited for: 11 -> 2; matrix products, arithmetic and copies ran while one was open for 12% -> 5% of each run, Pallas kernels for 0% -> 0%
where the time goes in v1:
time: 191 us
  Pallas kernels  153 us (80%)
  local copies, waits for them, and re-layouts  12.8 us (7%)
  starting transfers between devices  11 us (6%)
  waiting for transfers between devices  6.91 us (4%)
  other arithmetic  6.75 us (4%)
    pallas_call x1, Pallas kernels, exchange_and_compute(): pl.pallas_call(kernel, out_shape=(jax.ShapeDtypeStruct((32, 2 * D), BF16)...  153 us
    unnamed x7, local copies, waits for them, and re-layouts  7.5 us
    all_to_all x1, starting transfers between devices, on_device(): lax.all_to_all(rows, 'frame', split_axis=0, concat_axis=0, tiled=True)  7.34 us
    all_to_all x1, waiting for transfers between devices, on_device(): lax.all_to_all(sums.reshape(16, 2, 2 * D), 'frame', split_axis=0, concat_...  6.02 us
  transfers between devices with their start and end apart: 2, of which 2 were waited for; matrix products, arithmetic and copies ran while one was open for 5% of the time, Pallas kernels for 0%

profile of v1, /device:TPU:1, one launch (start us, length us, event | category | flops | bytes accessed | tf_op | source)
XLA Modules:
  0.0 190.9 jit_solution(9719852690874993284)
XLA Ops:
  0.6 1.2 fusion.9
  1.9 0.8 broadcast_add_fusion
  2.7 1.5 fusion.4
  4.2 1.2 pad_maximum_fusion
  5.4 7.3 %all-to-all-start = ((bf16[16,2,6144]{2,1,0:T(2,128)(2,1)}), bf16[16,2,6144]{2,1,0:T(2,128)(2,1)S(1)}, u32[]{:S(2)}, u32[]{:S(2)}) async-start(bf16[16,2,6144]{2,1,0:T(2,128)(2,1)} %bitcast), calls=%async_computation | async-start | bytes 786432 | tf_op jit(solution)/shard_map/all_to_all | solution.py:448
  12.7 7.5 %copy.9 = bf16[384,8,4,256]{3,1,2,0:T(8,128)(2,1)} copy(bf16[384,8,4,256]{3,2,1,0:T(4,128)(2,1)} %bitcast.5) | data formatting | bytes 12582912
  20.2 0.0 copy-start
  20.2 0.0 copy-start.1
  20.2 0.0 copy-start.2
  20.2 0.9 all-to-all-done
  21.1 0.9 reshape.40.x0
  22.0 152.8 %shard_map.85 = (bf16[32,6144]{1,0:T(8,128)(2,1)}, f32[192,1024]{1,0:T(8,128)}) custom-call(bf16[32,6144]{1,0:T(8,128)(2,1)} %reshape.40.x0, bf16[3072,1024]{1,0:T(8,128)(2,1)} %bitcast.4), custom_call_target="tpu_custom_call" | custom-call | tf_op jit(solution)/shard_map/pallas_call | solution.py:401
  174.8 2.0 %reshape.42 = bf16[16,2,6144]{2,1,0:T(2,128)(2,1)} reshape(bf16[32,6144]{1,0:T(8,128)(2,1)} %get-tuple-element.5) | data formatting | bytes 786432 | tf_op jit(solution)/shard_map/reshape | solution.py:453
  176.8 3.7 %all-to-all-start.1 = ((bf16[16,2,6144]{2,1,0:T(2,128)(2,1)}), bf16[16,2,6144]{2,1,0:T(2,128)(2,1)S(1)}, u32[]{:S(2)}, u32[]{:S(2)}) async-start(bf16[16,2,6144]{2,1,0:T(2,128)(2,1)} %reshape.42), calls=%async_computation.1 | async-start | bytes 786432 | tf_op jit(solution)/shard_map/all_to_all | solution.py:452
  180.5 2.4 %reshape.44 = f32[192,4,256]{2,1,0:T(4,128)} reshape(f32[192,1024]{1,0:T(8,128)} %get-tuple-element.6) | data formatting | bytes 1572864 | tf_op jit(solution)/shard_map/reshape | solution.py:462
  182.9 6.0 %all-to-all-done.1 = bf16[16,2,6144]{2,1,0:T(2,128)(2,1)S(1)} async-done(((bf16[16,2,6144]{2,1,0:T(2,128)(2,1)}), bf16[16,2,6144]{2,1,0:T(2,128)(2,1)S(1)}, u32[]{:S(2)}, u32[]{:S(2)}) %all-to-all-start.1) | async-done | bytes 393248 | tf_op jit(solution)/shard_map/all_to_all | solution.py:452
  188.9 0.0 copy-done
  188.9 0.5 fusion.5
  189.4 0.0 copy-done.1
  189.4 0.0 copy-done.2
  189.4 1.5 fusion.11
  (2 shorter events, 0.0 us)
Async XLA Ops:
  5.4 15.7 %all-to-all-start = ((bf16[16,2,6144]{2,1,0:T(2,128)(2,1)}), bf16[16,2,6144]{2,1,0:T(2,128)(2,1)S(1)}, u32[]{:S(2)}, u32[]{:S(2)}) async-start(bf16[16,2,6144]{2,1,0:T(2,128)(2,1)} %bitcast), calls=%async_computation | async-start | bytes 786432 | tf_op jit(solution)/shard_map/all_to_all | solution.py:448
  20.2 168.7 %copy-start = (bf16[8,2,2,3072]{3,2,1,0:T(2,128)(2,1)S(1)}, bf16[8,2,2,3072]{3,2,1,0:T(2,128)(2,1)}, u32[]{:S(2)}) copy-start(bf16[8,2,2,3072]{3,2,1,0:T(2,128)(2,1)} %param.6) | copy-start | bytes 589828
  20.2 169.2 %copy-start.1 = (bf16[8,2,2,3072]{3,2,1,0:T(2,128)(2,1)S(1)}, bf16[8,2,2,3072]{3,2,1,0:T(2,128)(2,1)}, u32[]{:S(2)}) copy-start(bf16[8,2,2,3072]{3,2,1,0:T(2,128)(2,1)} %param.7) | copy-start | bytes 589828
  20.2 169.2 %copy-start.2 = (f32[2,2,3072]{2,1,0:T(2,128)S(1)}, f32[2,2,3072]{2,1,0:T(2,128)}, u32[]{:S(2)}) copy-start(f32[2,2,3072]{2,1,0:T(2,128)} %param.10) | copy-start | bytes 147460
  176.8 12.1 %all-to-all-start.1 = ((bf16[16,2,6144]{2,1,0:T(2,128)(2,1)}), bf16[16,2,6144]{2,1,0:T(2,128)(2,1)S(1)}, u32[]{:S(2)}, u32[]{:S(2)}) async-start(bf16[16,2,6144]{2,1,0:T(2,128)(2,1)} %reshape.42), calls=%async_computation.1 | async-start | bytes 786432 | tf_op jit(solution)/shard_map/all_to_all | solution.py:452

commit v2 on v1

--- a/solution.py
+++ b/solution.py
@@ -12,6 +12,7 @@
 BF16 = jnp.bfloat16
 F32 = jnp.float32
 MIB = 1024 * 1024
+SPLIT = 2432
 
 
 def dot(a, b, dims=((1,), (0,))):
@@ -135,9 +136,17 @@
             links.copy(piece(-1, 1), second(1, 1), back),
         )
 
+    def begin_far(self):
+        for made in self.far:
+            made.start()
+
+    def begin_own(self):
+        for made in self.own:
+            made.start()
+
     def begin(self):
-        for made in self.far + self.own:
-            made.start()
+        self.begin_far()
+        self.begin_own()
 
     def onward(self):
         for side, target in enumerate((self.piece(1, 0), self.piece(-1, 1))):
@@ -175,14 +184,27 @@
         for row in rows:
             row.begin()
 
-    def onward(row):
-        return row.onward
-
-    def end_rows():
-        for row in rows:
-            row.end()
-
-    return [begin] + [row.onward for row in rows] + [end_rows, column.begin, column.onward, column.end]
+    def end_far():
+        rows[0].end()
+        column.begin_far()
+
+    def end_near():
+        rows[1].end()
+        rows[2].end()
+        column.begin_own()
+
+    return [begin] + [row.onward for row in rows] + [end_far, end_near, rows[3].end, column.onward, column.end]
+
+
+def side_by_side(*lists):
+    def together(events):
+        def event():
+            for each in events:
+                each()
+
+        return event
+
+    return [together(events) for events in zip(*lists)]
 
 
 def softmax_rows(scores):
@@ -197,10 +219,12 @@
 
 
 def kernel(
-    x0, w_hbm, out, dw,
+    tokens_hbm, cotangent_hbm, shift_hbm, scale_hbm, gate_hbm, w_hbm, mixed, grad_tokens, dw,
+    tokens, cotangent, shift, scale, gate, normed_in, scaled_in, branch_in, grad_in,
+    land_normed, land_scaled, stage, parted, raw, stage_w,
     xall, w, qkv, grad_att, dall, turned, probs, branch, grad, dpart,
     land1b, land2b, land1g, land2g, land_core, land1y, land2y, land_z, flipped, core_out, core_in,
-    send_sems, recv_sems, local_sems,
+    send_sems, recv_sems, local_sems, out_sems, in_sems,
 ):
     f, m = lax.axis_index("frame"), lax.axis_index("mp")
     x, z = lax.rem(m, 4), lax.div(m, 4)
@@ -214,30 +238,154 @@
     links = Links(send_sems, recv_sems)
 
     own_rows = pl.ds(pl.multiple_of(m * 32, 32), 32)
-    take = pltpu.make_async_copy(x0, xall.at[own_rows, :], local_sems.at[0])
-    take.start()
-    weigh = pltpu.make_async_copy(w_hbm, w, local_sems.at[1])
-    weigh.start()
+    inputs = [
+        pltpu.make_async_copy(source, target, local_sems.at[5 + number])
+        for number, (source, target) in enumerate(
+            (
+                (tokens_hbm, tokens),
+                (cotangent_hbm, cotangent),
+                (shift_hbm, shift),
+                (scale_hbm, scale),
+                (gate_hbm, gate),
+            )
+        )
+    ]
+    for made in inputs:
+        made.start()
     barrier = pltpu.get_barrier_semaphore()
-    for ring in (ring_x, ring_z, ring_y):
+    for ring in (ring_x, ring_z):
         for step in (1, -1):
             pl.semaphore_signal(barrier, inc=1, device_id=ring.to(step), device_id_type=MESH)
-    for partner in (z_partner, core_partner):
-        pl.semaphore_signal(barrier, inc=1, device_id=partner, device_id_type=MESH)
-    pl.semaphore_wait(barrier, 8)
-    take.wait()
-
-    normed = gather_events(links, xall, slice(0, D), ring_z, ring_x)
-    scaled = gather_events(links, xall, slice(D, 2 * D), ring_z, ring_x)
-    sum_branch = scatter_events(links, branch, slice(0, D), ring_x, ring_z, land1b, land2b)
-    sum_grad = scatter_events(links, grad, slice(0, D), ring_x, ring_z, land1g, land2g)
+
+    @pl.loop(1, 16)
+    def _(step):
+        pl.semaphore_signal(
+            barrier, inc=1, device_id=(lax.rem(f + step, 16), m), device_id_type=MESH
+        )
+
+    weigh = pltpu.make_async_copy(w_hbm, raw, local_sems.at[4])
+    weigh.start()
+    for made in inputs:
+        made.wait()
+
+    def unit_rows(part):
+        values = tokens[part].astype(F32)
+        inverse_rms = lax.rsqrt(jnp.mean(values * values, axis=-1, keepdims=True) + EPSILON)
+        return values * inverse_rms, inverse_rms
+
+    @pl.loop(0, 8)
+    def _(patch):
+        for clip in range(2):
+            part = 2 * patch + clip
+            unit, _ = unit_rows(part)
+            normed_in[part] = (unit * (1.0 + scale[clip]) + shift[clip]).astype(BF16)
+            scaled_in[part] = (cotangent[part].astype(F32) * gate[clip]).astype(BF16)
+
+    def mix():
+        @pl.loop(0, 8)
+        def _(patch):
+            for clip in range(2):
+                part = 2 * patch + clip
+                mixed[part] = (
+                    tokens[part].astype(F32) + gate[clip] * branch_in[part].astype(F32)
+                ).astype(BF16)
+
+    def grad_back():
+        @pl.loop(0, 8)
+        def _(patch):
+            for clip in range(2):
+                part = 2 * patch + clip
+                unit, inverse_rms = unit_rows(part)
+                grad_unit = grad_in[part].astype(F32) * (1.0 + scale[clip])
+                correction = jnp.mean(grad_unit * unit, axis=-1, keepdims=True)
+                grad_tokens[part] = (
+                    cotangent[part].astype(F32) + inverse_rms * (grad_unit - unit * correction)
+                ).astype(BF16)
+
+    pl.semaphore_wait(barrier, 19)
+
+    def exchange(number, source, target):
+        def copy(step):
+            to = lax.rem(f + step, 16)
+            return pltpu.make_async_remote_copy(
+                src_ref=source.at[to],
+                dst_ref=target.at[f],
+                send_sem=out_sems.at[number, step - 1],
+                recv_sem=in_sems.at[number, step - 1],
+                device_id=(to, m),
+                device_id_type=MESH,
+            )
+
+        def here():
+            return pltpu.make_async_copy(source.at[f], target.at[f], local_sems.at[number])
+
+        def begin():
+            @pl.loop(1, 16)
+            def _(step):
+                copy(step).start()
+
+            here().start()
+
+        def end():
+            @pl.loop(1, 16)
+            def _(step):
+                copy(step).wait()
+
+            here().wait()
+
+        return begin, end
+
+    def assemble(landed, base):
+        for part in range(16):
+            stage[2 * part : 2 * part + 2, :] = landed[part].astype(F32)
+        xall[own_rows, base : base + D] = stage[...].astype(BF16)
+
+    def part_rows(buffer, number):
+        stage[...] = buffer[own_rows, :].astype(F32)
+        for part in range(16):
+            parted[number, part] = stage[2 * part : 2 * part + 2, :].astype(BF16)
+
+    normed_begin, normed_end = exchange(0, normed_in, land_normed)
+    scaled_begin, scaled_end = exchange(1, scaled_in, land_scaled)
+    branch_begin, branch_end = exchange(2, parted.at[0], branch_in)
+    grad_begin, grad_end = exchange(3, parted.at[1], grad_in)
+
+    def arrange(first, last):
+        def event():
+            @pl.loop(first, last)
+            def _(part):
+                stage_w[...] = raw[pl.ds(pl.multiple_of(part * 512, 512), 512), :].astype(F32)
+                rows = pl.ds(pl.multiple_of(part * 64, 64), 64)
+                for half in range(2):
+                    for slot in range(4):
+                        place = slot * 256 + half * HD
+                        w[rows, place : place + HD] = stage_w[
+                            pl.ds(4 * half + slot, 64, stride=8), :
+                        ].astype(BF16)
+
+        return event
+
+    def gather(base):
+        return side_by_side(
+            gather_events(links, xall, slice(base, base + SPLIT), ring_z, ring_x),
+            gather_events(links, xall, slice(base + SPLIT, base + D), ring_x, ring_z),
+        )
+
+    def scatter(buffer, land1, land2):
+        return side_by_side(
+            scatter_events(links, buffer, slice(0, SPLIT), ring_x, ring_z, land1, land2),
+            scatter_events(links, buffer, slice(SPLIT, D), ring_z, ring_x, land1, land2),
+        )
+
+    normed, scaled = gather(0), gather(D)
+    sum_branch, sum_grad = scatter(branch, land1b, land2b), scatter(grad, land1g, land2g)
 
     def chip_columns(y_to, zl_to):
         return pl.ds(pl.multiple_of(zl_to * 1536 + y_to * 384, 128), 384)
 
     mine = pl.multiple_of(core * 512, 512)
     theirs = pl.multiple_of(other * 512, 512)
-    chunks = [(step, side) for step in (2, 1, -1, 0) for side in (1, 0)]
+    chunks = [(step, side) for side in (1, 0) for step in (2, 1, -1, 0)]
     core_copies = {}
     for step, side in chunks:
         columns = chip_columns(ring_y.at(step), lax.rem(zl + side, 2))
@@ -354,59 +502,78 @@
         flipped[...] = total.T
         core_out[...] = flipped[pl.ds(pl.multiple_of(other * 192, 192), 192), :].astype(BF16)
         core_copy.start()
-        dw[:, pl.ds(mine, 512)] = flipped[pl.ds(pl.multiple_of(core * 192, 192), 192), :]
+        give(2 * core, flipped[pl.ds(pl.multiple_of(core * 192, 192), 192), :])
+
+    def give(slot, values):
+        for number in range(4):
+            place = pl.ds(4 * (number % 2) + slot + number // 2, 192, stride=8)
+            dw[place, :] = values[:, number * HD : number * HD + HD]
 
     def core_end():
         core_copy.wait_recv()
-        dw[:, pl.ds(theirs, 512)] = core_in[...].astype(F32)
+        give(2 * other, core_in[...].astype(F32))
 
     n, s, b, g = normed, scaled, sum_branch, sum_grad
     plan = [
-        *n[:5], s[0], *n[5:8], s[1], s[2], n[8],
-        weigh.wait,
+        normed_begin, scaled_begin, normed_end, lambda: assemble(land_normed, 0),
+        n[0],
+        scaled_end, lambda: assemble(land_scaled, D),
+        weigh.wait, n[1], n[2], arrange(0, 8), n[3], n[4], arrange(8, 16), s[0], n[5], arrange(16, 24), n[6],
+        arrange(24, 32), n[7], arrange(32, 40), s[1], s[2], arrange(40, 48), n[8],
         lambda: project(0), s[3], lambda: project(1), s[4], lambda: project(2), s[5],
-        attend, s[6], all_branch, s[7],
-        b[0],
+        attend, s[6], all_branch, s[7], b[0],
         s[8],
-        back_project, b[1], attend_back, b[2], all_grad, g[0], b[3], b[4],
-        turn,
-        *[weight_chunk(*chunk) for chunk in chunks[:4]],
-        b[5], b[6],
-        *[core_sum(*chunk) for chunk in chunks[:2]],
-        *[weight_chunk(*chunk) for chunk in chunks[4:]],
-        g[1], g[2],
-        *[core_sum(*chunk) for chunk in chunks[2:6]],
-        y_sums[1].begin, y_sums[0].begin,
-        b[7], g[3], g[4],
-        *[core_sum(*chunk) for chunk in chunks[6:]],
-        b[8],
-        y_sums[1].onward, y_sums[0].onward,
-        g[5], g[6],
+        back_project, b[1], attend_back, b[2], turn,
+        *[weight_chunk(*chunk) for chunk in chunks[:4]], b[3],
+        *[weight_chunk(*chunk) for chunk in chunks[4:]], b[4],
+        all_grad, g[0], b[5], b[6],
+        *[core_sum(*chunk) for chunk in chunks[:4]], y_sums[1].begin,
+        b[7],
+        *[core_sum(*chunk) for chunk in chunks[4:]], y_sums[0].begin,
+        b[8], g[1], g[2],
+        y_sums[1].onward,
+        b[9], lambda: part_rows(branch, 0), branch_begin,
+        g[3], g[4], y_sums[0].onward,
+        g[5], g[6], g[7],
         y_sums[1].end, z_copy.start,
-        g[7],
-        y_sums[0].end,
-        z_end,
         g[8],
+        y_sums[0].end, z_end,
+        g[9], lambda: part_rows(grad, 1), grad_begin,
         core_end,
+        branch_end, mix, grad_end, grad_back,
     ]
     for event in plan:
         event()
-    out[:, :D] = branch[own_rows, :]
-    out[:, D:] = grad[own_rows, :]
     links.drain()
 
 
-def exchange_and_compute(x0, weights):
-    copies = 160
+def attention_block(tokens, cotangent, shift, scale, gate, weights):
+    copies = 224
     return pl.pallas_call(
         kernel,
         out_shape=(
-            jax.ShapeDtypeStruct((32, 2 * D), BF16),
-            jax.ShapeDtypeStruct((192, 1024), F32),
+            jax.ShapeDtypeStruct((16, 2, D), BF16),
+            jax.ShapeDtypeStruct((16, 2, D), BF16),
+            jax.ShapeDtypeStruct((1536, HD), F32),
         ),
-        in_specs=[pl.BlockSpec(memory_space=pl.ANY)] * 2,
-        out_specs=[pl.BlockSpec(memory_space=pltpu.VMEM)] * 2,
+        in_specs=[pl.BlockSpec(memory_space=pl.ANY)] * 6,
+        out_specs=[pl.BlockSpec(memory_space=pltpu.VMEM)] * 3,
         scratch_shapes=[
+            pltpu.VMEM((16, 2, D), BF16),
+            pltpu.VMEM((16, 2, D), BF16),
+            pltpu.VMEM((2, 2, D), F32),
+            pltpu.VMEM((2, 2, D), F32),
+            pltpu.VMEM((2, 2, D), F32),
+            pltpu.VMEM((16, 2, D), BF16),
+            pltpu.VMEM((16, 2, D), BF16),
+            pltpu.VMEM((16, 2, D), BF16),
+            pltpu.VMEM((16, 2, D), BF16),
+            pltpu.VMEM((16, 2, D), BF16),
+            pltpu.VMEM((16, 2, D), BF16),
+            pltpu.VMEM((32, D), F32),
+            pltpu.VMEM((2, 16, 2, D), BF16),
+            pltpu.VMEM((24576, HD), BF16),
+            pltpu.VMEM((512, HD), F32),
             pltpu.VMEM((512, 2 * D), BF16),
             pltpu.VMEM((D, 1024), BF16),
             pltpu.VMEM((512, 768), BF16),
@@ -430,36 +597,23 @@
             pltpu.VMEM((192, 512), BF16),
             pltpu.SemaphoreType.DMA((copies,)),
             pltpu.SemaphoreType.DMA((copies,)),
-            pltpu.SemaphoreType.DMA((2,)),
+            pltpu.SemaphoreType.DMA((10,)),
+            pltpu.SemaphoreType.DMA((4, 15)),
+            pltpu.SemaphoreType.DMA((4, 15)),
         ],
         compiler_params=pltpu.CompilerParams(
             collective_id=0, has_side_effects=True, vmem_limit_bytes=60 * MIB
         ),
-    )(x0, weights)
+    )(tokens, cotangent, shift, scale, gate, weights)
 
 
 def on_device(tokens, cotangent, mod_shift, mod_scale, mod_gate, attn_weights):
-    values = tokens.astype(F32)
-    inverse_rms = lax.rsqrt(jnp.mean(values * values, axis=-1, keepdims=True) + EPSILON)
-    unit = values * inverse_rms
-    normed = (unit * (1.0 + mod_scale) + mod_shift).astype(BF16)
-    scaled = (cotangent.astype(F32) * mod_gate).astype(BF16)
-    rows = jnp.concatenate([normed, scaled], axis=-1).reshape(16, 2, 2 * D)
-    rows = lax.all_to_all(rows, "frame", split_axis=0, concat_axis=0, tiled=True)
-    sums, weight_grads = exchange_and_compute(
-        rows.reshape(32, 2 * D), attn_weights.reshape(D, 1024)
+    weights = attn_weights.reshape(D, 4, 2, HD).transpose(0, 2, 1, 3).reshape(8 * D, HD)
+    mixed, grad_tokens, weight_grads = attention_block(
+        tokens.reshape(16, 2, D), cotangent.reshape(16, 2, D), mod_shift, mod_scale, mod_gate, weights
     )
-    sums = lax.all_to_all(
-        sums.reshape(16, 2, 2 * D), "frame", split_axis=0, concat_axis=0, tiled=True
-    ).reshape(8, 2, 2, 2 * D)
-    branch, grad_normed = sums[..., :D].astype(F32), sums[..., D:].astype(F32)
-    mixed = (values + mod_gate * branch).astype(BF16)
-    grad_unit = grad_normed * (1.0 + mod_scale)
-    correction = jnp.mean(grad_unit * unit, axis=-1, keepdims=True)
-    grad_tokens = (
-        cotangent.astype(F32) + inverse_rms * (grad_unit - unit * correction)
-    ).astype(BF16)
-    return mixed, grad_tokens, weight_grads.reshape(192, 4, 256)
+    weight_grads = weight_grads.reshape(192, 2, 4, HD).transpose(0, 2, 1, 3).reshape(192, 4, 256)
+    return mixed.reshape(tokens.shape), grad_tokens.reshape(tokens.shape), weight_grads
 
 
 def solution(mesh):

time: 191 us -> 147 us (0.77)
  Pallas kernels: 153 us -> 141 us
  starting transfers between devices: 11 us -> 0 us
  local copies, waits for them, and re-layouts: 12.8 us -> 5.63 us
  waiting for transfers between devices: 6.91 us -> 0 us
  other arithmetic: 6.75 us -> 0 us
    pallas_call x1, Pallas kernels: 153 us -> 141 us  [attention_block(): pl.pallas_call(kernel, out_shape=(jax.ShapeDtypeStruct((16, 2, D), BF16),...]
    all_to_all x2 -> x0, starting transfers between devices: 11 us -> none  [the longest x1 7.34 us: on_device(): lax.all_to_all(rows, 'frame', split_axis=0, concat_axis=0, tiled=True)]
    all_to_all x2 -> x0, waiting for transfers between devices: 6.91 us -> none  [the longest x1 6.02 us: on_device(): lax.all_to_all(sums.reshape(16, 2, 2 * D), 'frame', split_axis=0, concat_...]
    reshape x3 -> x0, local copies, waits for them, and re-layouts: 5.26 us -> none  [the longest x1 2.37 us: on_device(): return (mixed, grad_tokens, weight_grads.reshape(192, 4, 256))]
    convert_element_type x2 -> x0, other arithmetic: 3.03 us -> none  [the longest x1 1.51 us: on_device(): grad_tokens = (cotangent.astype(F32) + inverse_rms * (grad_unit - unit *...]
    unnamed x7 -> x3, local copies, waits for them, and re-layouts: 7.5 us -> 5.63 us
  transfers between devices with their start and end apart: 2 -> 0, of which waited for: 2 -> 0; matrix products, arithmetic and copies ran while one was open for 5% -> 0% of each run, Pallas kernels for 0% -> 0%
where the time goes in v2:
time: 147 us
  Pallas kernels  141 us (96%)
  local copies, waits for them, and re-layouts  5.63 us (4%)
    pallas_call x1, Pallas kernels, attention_block(): pl.pallas_call(kernel, out_shape=(jax.ShapeDtypeStruct((16, 2, D), BF16),...  141 us
    unnamed x3, local copies, waits for them, and re-layouts  5.63 us

profile of v2, /device:TPU:1, one launch (start us, length us, event | category | flops | bytes accessed | tf_op | source)
XLA Modules:
  0.0 147.1 jit_solution(3173812998204755802)
XLA Ops:
  0.6 140.8 %shard_map.85 = (bf16[16,2,3072]{2,1,0:T(2,128)(2,1)}, bf16[16,2,3072]{2,1,0:T(2,128)(2,1)}, f32[1536,128]{1,0:T(8,128)}) custom-call(bf16[16,2,3072]{2,1,0:T(2,128)(2,1)} %bitcast.18, bf16[16,2,3072]{2,1,0:T(2,128)(2,1)} %bitcast.19, f32[2,2,3072]{2,1,0:T(2,128)} %shift_hbm.1, f32[2,2,3072]{2,1,0:T(2,128)} %scale_hbm.1, f32[2,2,3072]{2,1,0:T(2,128)} %gate_hbm.1, ...), custom_call_target="tpu_custom_call" | custom-call | tf_op jit(solution)/shard_map/pallas_call | solution.py:552
  141.4 1.7 %copy.14 = bf16[8,2,2,3072]{3,2,1,0:T(2,128)(2,1)} copy(bf16[8,2,2,3072]{3,2,1,0:T(2,128)(2,1)} %bitcast.17) | data formatting | bytes 393216
  143.2 1.7 %copy.15 = bf16[8,2,2,3072]{3,2,1,0:T(2,128)(2,1)} copy(bf16[8,2,2,3072]{3,2,1,0:T(2,128)(2,1)} %bitcast.16) | data formatting | bytes 393216
  144.9 2.1 %copy.16 = f32[192,4,256]{2,1,0:T(4,128)} copy(f32[192,4,256]{2,1,0:T(4,128)} %bitcast.15) | data formatting | bytes 1572864

commit v3 on v2

v3 whole, which is shorter than its diff:
```python
from types import SimpleNamespace

import jax
import jax.numpy as jnp
from jax import lax
from jax.experimental import pallas as pl
from jax.experimental.pallas import tpu as pltpu
from jax.sharding import PartitionSpec as P

HD = 128
D = 3072
EPSILON = 1e-06
MESH = pl.DeviceIdType.MESH
BF16 = jnp.bfloat16
F32 = jnp.float32
MIB = 1024 * 1024
SPLIT = 2432


def dot(a, b, dims=((1,), (0,))):
    return lax.dot_general(a, b, (dims, ((), ())), preferred_element_type=F32)


NT = ((1,), (1,))
TN = ((0,), (0,))


class Ring:
    def __init__(self, index, device, stride):
        self.index, self.device, self.stride = index, device, stride

    def at(self, step):
        return lax.rem(self.index + (step + 4), 4)

    def to(self, step):
        return self.device(self.at(step))


class Links:
    def __init__(self, send_sems, recv_sems):
        self.send_sems, self.recv_sems = send_sems, recv_sems
        self.groups, self.sends = 0, []

    def send_group(self, whole):
        self.sends.append(whole)
        return len(self.sends) - 1

    def recv_group(self):
        self.groups += 1
        return self.groups - 1

    def copy(self, source, target, device, send, recv):
        return pltpu.make_async_remote_copy(
            src_ref=source,
            dst_ref=target,
            send_sem=self.send_sems.at[send],
            recv_sem=self.recv_sems.at[recv],
            device_id=device,
            device_id_type=MESH,
        )

    def wait(self, recv, whole):
        pltpu.make_async_copy(whole, whole, self.recv_sems.at[recv]).wait()

    def drain(self):
        for send, whole in enumerate(self.sends):
            pltpu.make_async_copy(whole, whole, self.send_sems.at[send]).wait()


def block_rows(first, second, one, two, half):
    block = first.at(one) * first.stride + second.at(two) * second.stride
    start = block * 32 + (0 if half is None else 16 * half)
    size = 32 if half is None else 16
    return pl.ds(pl.multiple_of(start, size), size)


def gather_steps(links, send, buffer, columns, first, second):
    class Group:
        def __init__(self, rows, *moves):
            self.whole, self.recv = buffer.at[0:rows, columns], links.recv_group()
            self.copies = []
            for ring, step, one, two, half in moves:
                part = buffer.at[block_rows(first, second, one, two, half), columns]
                self.copies.append(links.copy(part, part, ring.to(step), send, self.recv))

        def start(self):
            for made in self.copies:
                made.start()

        def wait(self):
            links.wait(self.recv, self.whole)

    places = (0, -1, 1, 2)
    ahead = Group(32, (first, 1, 0, 0, None))
    back = Group(32, (first, -1, 0, 0, None))
    across = Group(32, (first, 1, -1, 0, 0), (first, -1, 1, 0, 1))
    near = {one: Group(64, (second, 1, one, 0, None), (second, -1, one, 0, None)) for one in places}
    far = Group(
        128, *[move for one in places for move in ((second, 1, one, -1, 0), (second, -1, one, 1, 1))]
    )

    def begin():
        for group in (ahead, back, near[0]):
            group.start()

    def from_behind():
        ahead.wait()
        across.copies[0].start()
        near[-1].start()

    def from_ahead():
        back.wait()
        across.copies[1].start()
        near[1].start()

    def from_across():
        across.wait()
        near[2].start()

    def onward(place):
        def event():
            near[places[place]].wait()
            far.copies[2 * place].start()
            far.copies[2 * place + 1].start()

        return event

    return SimpleNamespace(
        begin=begin,
        behind=from_behind,
        ahead=from_ahead,
        across=from_across,
        on_own=onward(0),
        on_behind=onward(1),
        on_ahead=onward(2),
        on_across=onward(3),
        end=far.wait,
    )


def add_to(target, *others):
    total = target[...].astype(F32)
    for other in others:
        total = total + other[...].astype(F32)
    target[...] = total.astype(target.dtype)


class RingSum:
    def __init__(self, links, send, ring, piece, first, second):
        self.links, self.piece, self.first, self.second = links, piece, first, second
        ahead, back = ring.to(1), ring.to(-1)
        self.early, self.late = links.recv_group(), links.recv_group()

        def copy(source, target, device, recv):
            return links.copy(source, target, device, send, recv)

        self.far = (
            copy(piece(2, 0), first(0), ahead, self.early),
            copy(piece(2, 1), first(1), back, self.early),
        )
        self.own = (
            copy(piece(1, 1), second(0, 1), ahead, self.late),
            copy(piece(-1, 0), second(1, 0), back, self.late),
        )
        self.summed = (
            copy(piece(1, 0), second(0, 0), ahead, self.late),
            copy(piece(-1, 1), second(1, 1), back, self.late),
        )

    def begin_far(self):
        for made in self.far:
            made.start()

    def begin_own(self):
        for made in self.own:
            made.start()

    def onward(self):
        self.links.wait(self.early, self.first(None))
        for side, target in enumerate((self.piece(1, 0), self.piece(-1, 1))):
            add_to(target, self.first(side))
            self.summed[side].start()

    def end(self):
        self.links.wait(self.late, self.second(None, None))
        for half in range(2):
            add_to(self.piece(0, half), self.second(0, half), self.second(1, half))


def sides(land, *rest):
    def view(side, half=None):
        if side is None:
            return land.at[(slice(None), slice(None), *rest)]
        if half is None:
            return land.at[(side, slice(None), *rest)]
        size = land.shape[1] // 2
        return land.at[(side, slice(size * half, size * half + size), *rest)]

    return view


def scatter_steps(links, send, buffer, columns, first, second, land1, land2):
    def over_first(slot, two):
        return RingSum(
            links,
            send,
            first,
            lambda one, half: buffer.at[block_rows(first, second, one, two, half), columns],
            sides(land1.at[slot], columns),
            sides(land2.at[slot], columns),
        )

    rows = [over_first(slot, two) for slot, two in enumerate((2, -1, 1, 0))]
    column = RingSum(
        links,
        send,
        second,
        lambda two, half: buffer.at[block_rows(first, second, 0, two, half), columns],
        sides(land1.at[4], columns),
        sides(land2.at[4], columns),
    )

    return [*rows, column]


def softmax_rows(scores):
    shifted = jnp.exp(scores - jnp.max(scores, axis=-1, keepdims=True))
    return shifted / jnp.sum(shifted, axis=-1, keepdims=True)


def same_block():
    rows = lax.broadcasted_iota(jnp.int32, (HD, HD), 0)
    columns = lax.broadcasted_iota(jnp.int32, (HD, HD), 1)
    return (rows >> 5) == (columns >> 5)


def kernel(
    tokens_hbm, cotangent_hbm, shift_hbm, scale_hbm, gate_hbm, w_hbm, mixed, grad_tokens, dw,
    tokens, cotangent, shift, scale, gate, normed_in, scaled_in, branch_in, grad_in,
    land_normed, land_scaled, stage, parted, raw, stage_w,
    xall, w, qkv, grad_att, dall, turned, probs, branch, grad, dpart,
    land1b, land2b, land1g, land2g, land_core, land1y, land2y, land_z, flipped, core_out, core_in,
    send_sems, recv_sems, local_sems, out_sems, in_sems,
):
    f, m = lax.axis_index("frame"), lax.axis_index("mp")
    x, z = lax.rem(m, 4), lax.div(m, 4)
    core, y, zl = lax.rem(f, 2), lax.rem(lax.div(f, 2), 4), lax.div(f, 8)
    other = 1 - core
    ring_x = Ring(x, lambda to: (f, z * 4 + to), 1)
    ring_z = Ring(z, lambda to: (f, to * 4 + x), 4)
    ring_y = Ring(y, lambda to: (zl * 8 + to * 2 + core, m), 0)
    z_partner = ((1 - zl) * 8 + y * 2 + core, m)
    core_partner = (zl * 8 + y * 2 + other, m)
    links = Links(send_sems, recv_sems)

    own_rows = pl.ds(pl.multiple_of(m * 32, 32), 32)
    inputs = [
        pltpu.make_async_copy(source, target, local_sems.at[5 + number])
        for number, (source, target) in enumerate(
            (
                (tokens_hbm, tokens),
                (cotangent_hbm, cotangent),
                (shift_hbm, shift),
                (scale_hbm, scale),
                (gate_hbm, gate),
            )
        )
    ]
    for made in inputs:
        made.start()
    barrier = pltpu.get_barrier_semaphore()
    for ring in (ring_x, ring_z):
        for step in (1, -1):
            pl.semaphore_signal(barrier, inc=1, device_id=ring.to(step), device_id_type=MESH)

    @pl.loop(1, 16)
    def _(step):
        pl.semaphore_signal(
            barrier, inc=1, device_id=(lax.rem(f + step, 16), m), device_id_type=MESH
        )

    weigh = pltpu.make_async_copy(w_hbm, raw, local_sems.at[4])
    weigh.start()
    for made in inputs:
        made.wait()

    def total(values):
        eight = values[0:8]
        for tile in range(1, 6):
            eight = eight + values[8 * tile : 8 * tile + 8]
        eight = eight + pltpu.roll(eight, 2, 0)
        eight = eight + pltpu.roll(eight, 4, 0)
        eight = jnp.sum(eight, axis=-1, keepdims=True)
        return jnp.concatenate([eight] * 6, axis=0)

    def part_of(patch, clip):
        return pl.ds(pl.multiple_of((2 * patch + clip) * 48, 48), 48)

    def of_clip(clip):
        return slice(48 * clip, 48 * clip + 48)

    def unit_rows(rows):
        values = tokens[rows, :].astype(F32)
        inverse_rms = lax.rsqrt(total(values * values) * (1.0 / D) + EPSILON)
        return values * inverse_rms, inverse_rms

    @pl.loop(0, 8)
    def _(patch):
        for clip in range(2):
            rows, own = part_of(patch, clip), of_clip(clip)
            unit, _ = unit_rows(rows)
            normed_in[rows, :] = (unit * (1.0 + scale[own, :]) + shift[own, :]).astype(BF16)
            scaled_in[rows, :] = (cotangent[rows, :].astype(F32) * gate[own, :]).astype(BF16)

    def mix():
        @pl.loop(0, 8)
        def _(patch):
            for clip in range(2):
                rows, own = part_of(patch, clip), of_clip(clip)
                mixed[rows, :] = (
                    tokens[rows, :].astype(F32) + gate[own, :] * branch_in[rows, :].astype(F32)
                ).astype(mixed.dtype)

    def grad_back():
        @pl.loop(0, 8)
        def _(patch):
            for clip in range(2):
                rows, own = part_of(patch, clip), of_clip(clip)
                unit, inverse_rms = unit_rows(rows)
                grad_unit = grad_in[rows, :].astype(F32) * (1.0 + scale[own, :])
                correction = total(grad_unit * unit) * (1.0 / D)
                grad_tokens[rows, :] = (
                    cotangent[rows, :].astype(F32) + inverse_rms * (grad_unit - unit * correction)
                ).astype(grad_tokens.dtype)

    pl.semaphore_wait(barrier, 19)

    def exchange(number, source, target):
        def part(index):
            return pl.ds(pl.multiple_of(index * 48, 48), 48)

        def copy(step):
            to = lax.rem(f + step, 16)
            return pltpu.make_async_remote_copy(
                src_ref=source.at[part(to)],
                dst_ref=target.at[part(f)],
                send_sem=out_sems.at[number],
                recv_sem=in_sems.at[number],
                device_id=(to, m),
                device_id_type=MESH,
            )

        def here():
            return pltpu.make_async_copy(source.at[part(f)], target.at[part(f)], local_sems.at[number])

        def begin():
            @pl.loop(1, 16)
            def _(step):
                copy(step).start()

            here().start()

        def end():
            pltpu.make_async_copy(target.at[0:720], target.at[0:720], in_sems.at[number]).wait()
            here().wait()

        def sent():
            pltpu.make_async_copy(source.at[0:720], source.at[0:720], out_sems.at[number]).wait()

        sent_all.append(sent)
        return begin, end

    def assemble(landed, base):
        stage[...] = landed[...].astype(F32)
        for tile in range(24):
            for frame in range(2):
                xall[
                    pl.ds(pl.multiple_of(m * 32 + 16 * frame, 16), 16),
                    base + HD * tile : base + HD * tile + HD,
                ] = stage[pl.ds(2 * tile + frame, 16, stride=48), :].astype(BF16)

    def part_rows(buffer, number):
        for tile in range(24):
            for frame in range(2):
                stage[pl.ds(2 * tile + frame, 16, stride=48), :] = buffer[
                    pl.ds(pl.multiple_of(m * 32 + 16 * frame, 16), 16), HD * tile : HD * tile + HD
                ].astype(F32)
        parted[number] = stage[...].astype(BF16)

    sent_all = []
    normed_begin, normed_end = exchange(0, normed_in, land_normed)
    scaled_begin, scaled_end = exchange(1, scaled_in, land_scaled)
    branch_begin, branch_end = exchange(2, parted.at[0], branch_in)
    grad_begin, grad_end = exchange(3, parted.at[1], grad_in)

    def arrange(first, last):
        def event():
            @pl.loop(first, last)
            def _(part):
                stage_w[...] = raw[pl.ds(pl.multiple_of(part * 512, 512), 512), :].astype(F32)
                rows = pl.ds(pl.multiple_of(part * 64, 64), 64)
                for half in range(2):
                    for slot in range(4):
                        place = slot * 256 + half * HD
                        w[rows, place : place + HD] = stage_w[
                            pl.ds(4 * half + slot, 64, stride=8), :
                        ].astype(BF16)

        return event

    early, late = slice(0, SPLIT), slice(SPLIT, D)

    def gather(base):
        send = links.send_group(xall.at[0:480, base : base + D])
        return (
            gather_steps(links, send, xall, slice(base, base + SPLIT), ring_z, ring_x),
            gather_steps(links, send, xall, slice(base + SPLIT, base + D), ring_x, ring_z),
        )

    def scatter(buffer, *lands):
        send = links.send_group(buffer.at[0:480, :])
        return (
            scatter_steps(links, send, buffer, early, ring_x, ring_z, *lands),
            scatter_steps(links, send, buffer, late, ring_z, ring_x, *lands),
        )

    (na, nb), (sa, sb) = gather(0), gather(D)
    ba, bb = scatter(branch, land1b, land2b)
    ga, gb = scatter(grad, land1g, land2g)

    def chip_columns(y_to, zl_to):
        return pl.ds(pl.multiple_of(zl_to * 1536 + y_to * 384, 128), 384)

    mine = pl.multiple_of(core * 512, 512)
    theirs = pl.multiple_of(other * 512, 512)
    chunks = [(step, side) for side in (1, 0) for step in (2, 1, -1, 0)]
    core_copies, core_sends, first_core = {}, links.send_group(land_core), links.groups
    for step, side in chunks:
        columns = chip_columns(ring_y.at(step), lax.rem(zl + side, 2))
        core_copies[step, side] = links.copy(
            dpart.at[pl.ds(theirs, 512), columns], land_core.at[:, columns], core_partner,
            core_sends, links.recv_group(),
        )

    def over_y(side):
        zl_to = lax.rem(zl + side, 2)
        return RingSum(
            links,
            links.send_group(dpart.at[0:768, 0:768]),
            ring_y,
            lambda step, half: dpart.at[
                pl.ds(pl.multiple_of(mine + 256 * half, 256), 256), chip_columns(ring_y.at(step), zl_to)
            ],
            sides(land1y.at[side]),
            sides(land2y.at[side]),
        )

    y_sums = [over_y(0), over_y(1)]
    z_recv, core_recv = links.recv_group(), links.recv_group()
    z_copy = links.copy(
        dpart.at[pl.ds(mine, 512), chip_columns(y, 1 - zl)], land_z, z_partner,
        links.send_group(land_z), z_recv,
    )
    core_copy = links.copy(
        core_out, core_in, core_partner, links.send_group(core_in), core_recv
    )

    def project(slot):
        qkv[:, 256 * slot : 256 * slot + 256] = dot(
            xall[:, :D], w[:, 256 * slot : 256 * slot + 256]
        ).astype(BF16)

    def attend(group):
        def event():
            mask = same_block()
            rows = slice(group * HD, group * HD + HD)
            for head in range(2):
                query = qkv[rows, head * HD : head * HD + HD]
                key = qkv[rows, 256 + head * HD : 256 + head * HD + HD]
                value = qkv[rows, 512 + head * HD : 512 + head * HD + HD]
                scores = dot(query, key, NT) * (HD ** -0.5)
                attention = softmax_rows(jnp.where(mask, scores, -1e30))
                probs[group * 2 + head] = attention
                dall[rows, 768 + head * HD : 768 + head * HD + HD] = dot(
                    attention.astype(BF16), value
                ).astype(BF16)

        return event

    def branch_part(part):
        def event():
            @pl.loop(2 * part, 2 * part + 2)
            def _(step):
                rows = pl.ds(pl.multiple_of(step * 512, 512), 512)
                branch[:, rows] = dot(dall[:, 768:], w[rows, 768:], NT).astype(BF16)

        return event

    def back_project():
        grad_att[...] = dot(xall[:, D:], w[:, 768:]).astype(BF16)

    def attend_back(group):
        def event():
            rows = slice(group * HD, group * HD + HD)
            for head in range(2):
                low = slice(head * HD, head * HD + HD)
                query = qkv[rows, head * HD : head * HD + HD]
                key = qkv[rows, 256 + head * HD : 256 + head * HD + HD]
                value = qkv[rows, 512 + head * HD : 512 + head * HD + HD]
                incoming = grad_att[rows, low]
                attention = probs[group * 2 + head]
                grad_probs = dot(incoming, value, NT)
                inner = jnp.sum(grad_probs * attention, axis=-1, keepdims=True)
                grad_scores = (attention * (grad_probs - inner) * (HD ** -0.5)).astype(BF16)
                dall[rows, head * HD : head * HD + HD] = dot(grad_scores, key).astype(BF16)
                dall[rows, 256 + head * HD : 256 + head * HD + HD] = dot(
                    grad_scores, query, TN
                ).astype(BF16)
                dall[rows, 512 + head * HD : 512 + head * HD + HD] = dot(
                    attention.astype(BF16), incoming, TN
                ).astype(BF16)

        return event

    def grad_part(part):
        def event():
            @pl.loop(2 * part, 2 * part + 2)
            def _(step):
                rows = pl.ds(pl.multiple_of(step * 512, 512), 512)
                grad[:, rows] = dot(dall[:, :768], w[rows, :768], NT).astype(BF16)

        return event

    def turn():
        for part in range(8):
            turned[part * HD : part * HD + HD, :] = dall[:, part * HD : part * HD + HD].T

    def weight_chunk(step, side):
        def event():
            zl_to = lax.rem(zl + side, 2)
            columns = chip_columns(ring_y.at(step), zl_to)
            gated = pl.ds(pl.multiple_of(D + zl_to * 1536 + ring_y.at(step) * 384, 128), 384)
            dpart[:768, columns] = dot(turned[:768, :], xall[:, columns]).astype(BF16)
            dpart[768:, columns] = dot(turned[768:, :], xall[:, gated]).astype(BF16)
            core_copies[step, side].start()

        return event

    def core_sum(step, side):
        def event():
            columns = chip_columns(ring_y.at(step), lax.rem(zl + side, 2))
            links.wait(first_core + chunks.index((step, side)), land_core.at[:, columns])
            add_to(dpart.at[pl.ds(mine, 512), columns], land_core.at[:, columns])

        return event

    def z_end():
        links.wait(z_recv, land_z)
        columns = chip_columns(y, zl)
        total = dpart[pl.ds(mine, 512), columns].astype(F32) + land_z[...].astype(F32)
        flipped[...] = total.T
        core_out[...] = flipped[pl.ds(pl.multiple_of(other * 192, 192), 192), :].astype(BF16)
        core_copy.start()
        give(2 * core, flipped[pl.ds(pl.multiple_of(core * 192, 192), 192), :])

    def give(slot, values):
        for number in range(4):
            place = pl.ds(4 * (number % 2) + slot + number // 2, 192, stride=8)
            dw[place, :] = values[:, number * HD : number * HD + HD]

    def core_end():
        links.wait(core_recv, core_in)
        give(2 * other, core_in[...].astype(F32))

    def y_begin(side):
        def event():
            y_sums[side].begin_far()
            y_sums[side].begin_own()

        return event

    def in_turn(*steps):
        def event():
            for step in steps:
                step()

        return event

    take_scaled = in_turn(scaled_end, lambda: assemble(land_scaled, D))
    ar = [arrange(8 * part, 8 * part + 8) for part in range(6)]
    ar[0] = in_turn(weigh.wait, ar[0])
    pr = [lambda slot=slot: project(slot) for slot in range(3)]
    br, gr = ([make(part) for part in range(3)] for make in (branch_part, grad_part))
    at, ab = ([make(part) for part in range(4)] for make in (attend, attend_back))
    wc, cs = ([make(*chunk) for chunk in chunks] for make in (weight_chunk, core_sum))
    y_start = [y_begin(side) for side in range(2)]
    y_on = [each.onward for each in y_sums]
    y_end = [y_sums[0].end, in_turn(y_sums[1].end, z_copy.start)]
    give_branch = in_turn(lambda: part_rows(branch, 0), branch_begin)
    give_grad = in_turn(lambda: part_rows(grad, 1), grad_begin)
    take_branch, take_grad = in_turn(branch_end, mix), in_turn(grad_end, grad_back)

    plan = [
        na.begin, nb.begin, ar[0], ar[1], ar[2], ar[3], ar[4], ar[5], take_scaled, sa.begin, na.on_own,
        nb.behind, nb.ahead, sb.begin, na.ahead, na.behind, sa.on_own, nb.on_own, nb.across, sb.behind,
        sb.ahead, na.on_ahead, sa.behind, sa.ahead, nb.on_behind, na.on_behind, nb.on_ahead, sb.across,
        sb.on_own, na.across, sa.on_behind, nb.on_across, sa.on_ahead, sb.on_behind, sb.on_ahead,
        na.on_across, sa.across, sb.on_across, na.end, nb.end, pr[0], pr[1], pr[2], sa.on_across, at[0],
        at[1], at[2], at[3], br[0], br[1], br[2], ba[1].begin_own, bb[3].begin_own, ba[0].begin_far,
        bb[0].begin_far, ba[2].begin_own, bb[2].begin_far, ba[1].begin_far, ba[0].begin_own, bb[1].begin_far,
        bb[3].begin_far, ba[2].begin_far, bb[2].begin_own, bb[1].begin_own, sb.end, bb[0].begin_own, sa.end,
        back_project, ab[0], ab[1], ab[2], ab[3], gr[0], gr[1], gr[2], gb[3].begin_far, gb[2].begin_own,
        gb[1].begin_far, gb[3].begin_own, gb[2].begin_far, ga[0].begin_far, gb[0].begin_far, gb[1].begin_own,
        turn, wc[0], wc[1], wc[2], ba[0].onward, bb[0].onward, bb[3].onward, ga[0].begin_own, wc[3], wc[4],
        wc[5], ba[2].onward, cs[0], gb[0].begin_own, wc[6], wc[7], cs[1], ga[0].onward, cs[2], gb[1].onward,
        cs[3], y_start[1], ga[2].begin_far, gb[2].onward, cs[4], ba[1].onward, bb[2].onward, cs[5],
        gb[3].onward, ga[1].begin_far, cs[6], ba[0].end, ba[4].begin_far, gb[0].onward, cs[7], y_start[0],
        ga[2].begin_own, bb[0].end, ga[1].begin_own, bb[4].begin_far, bb[1].onward, bb[3].end, ba[2].end,
        gb[1].end, ga[0].end, ga[4].begin_far, gb[2].end, gb[4].begin_own, y_on[1], bb[2].end, ga[2].onward,
        gb[3].end, ba[1].end, ba[4].begin_own, ga[1].onward, ba[4].onward, gb[0].end, gb[4].begin_far,
        bb[1].end, bb[4].begin_own, ba[3].begin_own, bb[4].onward, ga[3].begin_far, y_on[0], ga[3].begin_own,
        ga[2].end, ga[1].end, ga[4].onward, ga[4].begin_own, gb[4].onward, ba[3].begin_far, bb[4].end,
        ga[3].onward, y_end[1], gb[4].end, ba[3].onward, y_end[0], ga[3].end, ga[4].end, give_grad,
        ba[3].end, ba[4].end, give_branch, z_end, take_grad, core_end, take_branch,
    ]
    normed_begin()
    scaled_begin()
    normed_end()
    assemble(land_normed, 0)
    for step in plan:
        step()
    links.drain()
    for sent in sent_all:
        sent()


def attention_block(tokens, cotangent, shift, scale, gate, weights):
    return pl.pallas_call(
        kernel,
        out_shape=(
            jax.ShapeDtypeStruct((768, HD), BF16),
            jax.ShapeDtypeStruct((768, HD), BF16),
            jax.ShapeDtypeStruct((1536, HD), F32),
        ),
        in_specs=[pl.BlockSpec(memory_space=pl.ANY)] * 6,
        out_specs=[pl.BlockSpec(memory_space=pltpu.VMEM)] * 3,
        scratch_shapes=[
            pltpu.VMEM((768, HD), BF16),
            pltpu.VMEM((768, HD), BF16),
            pltpu.VMEM((96, HD), F32),
            pltpu.VMEM((96, HD), F32),
            pltpu.VMEM((96, HD), F32),
            pltpu.VMEM((768, HD), BF16),
            pltpu.VMEM((768, HD), BF16),
            pltpu.VMEM((768, HD), BF16),
            pltpu.VMEM((768, HD), BF16),
            pltpu.VMEM((768, HD), BF16),
            pltpu.VMEM((768, HD), BF16),
            pltpu.VMEM((768, HD), F32),
            pltpu.VMEM((2, 768, HD), BF16),
            pltpu.VMEM((24576, HD), BF16),
            pltpu.VMEM((512, HD), F32),
            pltpu.VMEM((512, 2 * D), BF16),
            pltpu.VMEM((D, 1024), BF16),
            pltpu.VMEM((512, 768), BF16),
            pltpu.VMEM((512, 256), BF16),
            pltpu.VMEM((512, 1024), BF16),
            pltpu.VMEM((1024, 512), BF16),
            pltpu.VMEM((8, HD, HD), F32),
            pltpu.VMEM((512, D), BF16),
            pltpu.VMEM((512, D), BF16),
            pltpu.VMEM((1024, D), BF16),
            pltpu.VMEM((5, 2, 16, D), BF16),
            pltpu.VMEM((5, 2, 32, D), BF16),
            pltpu.VMEM((5, 2, 16, D), BF16),
            pltpu.VMEM((5, 2, 32, D), BF16),
            pltpu.VMEM((512, D), BF16),
            pltpu.VMEM((2, 2, 256, 384), BF16),
            pltpu.VMEM((2, 2, 512, 384), BF16),
            pltpu.VMEM((512, 384), BF16),
            pltpu.VMEM((384, 512), F32),
            pltpu.VMEM((192, 512), BF16),
            pltpu.VMEM((192, 512), BF16),
            pltpu.SemaphoreType.DMA((9,)),
            pltpu.SemaphoreType.DMA((86,)),
            pltpu.SemaphoreType.DMA((10,)),
            pltpu.SemaphoreType.DMA((4,)),
            pltpu.SemaphoreType.DMA((4,)),
        ],
        compiler_params=pltpu.CompilerParams(
            collective_id=0, has_side_effects=True, vmem_limit_bytes=60 * MIB
        ),
    )(tokens, cotangent, shift, scale, gate, weights)


def copy_kernel(*refs):
    half = len(refs) // 2
    for source, target in zip(refs[:half], refs[half:]):
        target[...] = source[...]


def copied(*arrays):
    return pl.pallas_call(
        copy_kernel,
        out_shape=[jax.ShapeDtypeStruct(each.shape, each.dtype) for each in arrays],
        in_specs=[pl.BlockSpec(memory_space=pltpu.VMEM)] * len(arrays),
        out_specs=[pl.BlockSpec(memory_space=pltpu.VMEM)] * len(arrays),
    )(*arrays)


def on_device(tokens, cotangent, mod_shift, mod_scale, mod_gate, attn_weights):
    weights = attn_weights.reshape(D, 4, 2, HD).transpose(0, 2, 1, 3).reshape(8 * D, HD)
    def tiles(values):
        lead = values.shape[:-2]
        return jnp.swapaxes(values.reshape(*lead, 2, 24, HD), -2, -3).reshape(-1, HD)

    def untiled(values):
        return jnp.swapaxes(values.reshape(8, 2, 24, 2, HD), -2, -3).reshape(8, 2, 2, D)

    mixed, grad_tokens, weight_grads = attention_block(
        tiles(tokens), tiles(cotangent), tiles(mod_shift), tiles(mod_scale), tiles(mod_gate), weights
    )
    mixed, grad_tokens, weight_grads = copied(mixed, grad_tokens, weight_grads)
    weight_grads = weight_grads.reshape(192, 2, 4, HD).transpose(0, 2, 1, 3).reshape(192, 4, 256)
    return untiled(mixed), untiled(grad_tokens), weight_grads


def solution(mesh):
    placed = (
        P("mp", None, "frame", None),
        P("mp", None, "frame", None),
        P(None, "frame", None),
        P(None, "frame", None),
        P(None, "frame", None),
        P(None, None, "mp"),
    )
    return jax.shard_map(
        on_device,
        mesh=mesh,
        in_specs=placed,
        out_specs=(
            P("mp", None, "frame", None),
            P("mp", None, "frame", None),
            P("frame", None, "mp"),
        ),
        check_vma=False,
    )
```

time: 147 us -> 130 us (0.88)
  Pallas kernels: 141 us -> 129 us
  local copies, waits for them, and re-layouts: 5.63 us -> 0 us
    pallas_call x1 -> x2, Pallas kernels: 141 us -> 129 us  [the longest x1 126 us: attention_block(): pl.pallas_call(kernel, out_shape=(jax.ShapeDtypeStruct((768, HD), BF16),...]
    unnamed x3 -> x0, local copies, waits for them, and re-layouts: 5.63 us -> none
where the time goes in v3:
time: 130 us; the launch traced here: 129 us
  Pallas kernels  129 us (99%)
    pallas_call x1, Pallas kernels, attention_block(): pl.pallas_call(kernel, out_shape=(jax.ShapeDtypeStruct((768, HD), BF16),...  126 us

profile of v3, /device:TPU:1, one launch (start us, length us, event | category | flops | bytes accessed | tf_op | source)
XLA Modules:
  0.0 129.4 jit_solution(7945306461978024389)
XLA Ops:
  0.6 126.4 %shard_map.85 = (bf16[768,128]{1,0:T(8,128)(2,1)}, bf16[768,128]{1,0:T(8,128)(2,1)}, f32[1536,128]{1,0:T(8,128)}) custom-call(bf16[768,128]{1,0:T(8,128)(2,1)} %bitcast.46, bf16[768,128]{1,0:T(8,128)(2,1)} %bitcast.47, f32[96,128]{1,0:T(8,128)} %bitcast.48, f32[96,128]{1,0:T(8,128)} %bitcast.49, f32[96,128]{1,0:T(8,128)} %bitcast.50, bf16[24576,128]{1,0:T(8,128)(2,1)} %bitcast.45), custom_call_target="tpu_custom_call" | custom-call | tf_op jit(solution)/shard_map/pallas_call | solution.py:638
  127.0 2.4 %shard_map.86 = (bf16[768,128]{1,0:T(8,128)(2,1)}, bf16[768,128]{1,0:T(8,128)(2,1)}, f32[1536,128]{1,0:T(8,128)}) custom-call(bf16[768,128]{1,0:T(8,128)(2,1)} %get-tuple-element.9.refs_0_, bf16[768,128]{1,0:T(8,128)(2,1)} %get-tuple-element.10.refs_1_, f32[1536,128]{1,0:T(8,128)} %get-tuple-element.11.refs_2_), custom_call_target="tpu_custom_call" | custom-call | tf_op jit(solution)/shard_map/pallas_call | solution.py:703

commit v4 on v3

--- a/solution.py
+++ b/solution.py
@@ -237,7 +237,7 @@
 def kernel(
     tokens_hbm, cotangent_hbm, shift_hbm, scale_hbm, gate_hbm, w_hbm, mixed, grad_tokens, dw,
     tokens, cotangent, shift, scale, gate, normed_in, scaled_in, branch_in, grad_in,
-    land_normed, land_scaled, stage, parted, raw, stage_w,
+    land_normed, land_scaled, stage, units, inverses, parted, raw, stage_w,
     xall, w, qkv, grad_att, dall, turned, probs, branch, grad, dpart,
     land1b, land2b, land1g, land2g, land_core, land1y, land2y, land_z, flipped, core_out, core_in,
     send_sems, recv_sems, local_sems, out_sems, in_sems,
@@ -302,15 +302,22 @@
     def unit_rows(rows):
         values = tokens[rows, :].astype(F32)
         inverse_rms = lax.rsqrt(total(values * values) * (1.0 / D) + EPSILON)
-        return values * inverse_rms, inverse_rms
+        return values * inverse_rms, jnp.broadcast_to(inverse_rms, values.shape)
 
     @pl.loop(0, 8)
     def _(patch):
         for clip in range(2):
             rows, own = part_of(patch, clip), of_clip(clip)
-            unit, _ = unit_rows(rows)
+            unit, inverse_rms = unit_rows(rows)
             normed_in[rows, :] = (unit * (1.0 + scale[own, :]) + shift[own, :]).astype(BF16)
-            scaled_in[rows, :] = (cotangent[rows, :].astype(F32) * gate[own, :]).astype(BF16)
+            units[rows, :], inverses[rows, :] = unit, inverse_rms
+
+    def gate_cotangent():
+        @pl.loop(0, 8)
+        def _(patch):
+            for clip in range(2):
+                rows, own = part_of(patch, clip), of_clip(clip)
+                scaled_in[rows, :] = (cotangent[rows, :].astype(F32) * gate[own, :]).astype(BF16)
 
     def mix():
         @pl.loop(0, 8)
@@ -326,7 +333,7 @@
         def _(patch):
             for clip in range(2):
                 rows, own = part_of(patch, clip), of_clip(clip)
-                unit, inverse_rms = unit_rows(rows)
+                unit, inverse_rms = units[rows, :], inverses[rows, :]
                 grad_unit = grad_in[rows, :].astype(F32) * (1.0 + scale[own, :])
                 correction = total(grad_unit * unit) * (1.0 / D)
                 grad_tokens[rows, :] = (
@@ -624,6 +631,7 @@
         ba[3].end, ba[4].end, give_branch, z_end, take_grad, core_end, take_branch,
     ]
     normed_begin()
+    gate_cotangent()
     scaled_begin()
     normed_end()
     assemble(land_normed, 0)
@@ -656,6 +664,8 @@
             pltpu.VMEM((768, HD), BF16),
             pltpu.VMEM((768, HD), BF16),
             pltpu.VMEM((768, HD), BF16),
+            pltpu.VMEM((768, HD), F32),
+            pltpu.VMEM((768, HD), F32),
             pltpu.VMEM((768, HD), F32),
             pltpu.VMEM((2, 768, HD), BF16),
             pltpu.VMEM((24576, HD), BF16),

time: 130 us -> 128 us (0.985)
  Pallas kernels: 129 us -> 127 us
    pallas_call x1, Pallas kernels: 126 us -> 125 us  [attention_block(): pl.pallas_call(kernel, out_shape=(jax.ShapeDtypeStruct((768, HD), BF16),...]
where the time goes in v4:
time: 128 us
  Pallas kernels  127 us (99%)
    pallas_call x1, Pallas kernels, attention_block(): pl.pallas_call(kernel, out_shape=(jax.ShapeDtypeStruct((768, HD), BF16),...  125 us

profile of v4, /device:TPU:1, one launch (start us, length us, event | category | flops | bytes accessed | tf_op | source)
XLA Modules:
  0.0 128.0 jit_solution(14345622137799462069)
XLA Ops:
  0.6 125.0 %shard_map.85 = (bf16[768,128]{1,0:T(8,128)(2,1)}, bf16[768,128]{1,0:T(8,128)(2,1)}, f32[1536,128]{1,0:T(8,128)}) custom-call(bf16[768,128]{1,0:T(8,128)(2,1)} %bitcast.46, bf16[768,128]{1,0:T(8,128)(2,1)} %bitcast.47, f32[96,128]{1,0:T(8,128)} %bitcast.48, f32[96,128]{1,0:T(8,128)} %bitcast.49, f32[96,128]{1,0:T(8,128)} %bitcast.50, bf16[24576,128]{1,0:T(8,128)(2,1)} %bitcast.45), custom_call_target="tpu_custom_call" | custom-call | tf_op jit(solution)/shard_map/pallas_call | solution.py:646
  125.6 2.4 %shard_map.86 = (bf16[768,128]{1,0:T(8,128)(2,1)}, bf16[768,128]{1,0:T(8,128)(2,1)}, f32[1536,128]{1,0:T(8,128)}) custom-call(bf16[768,128]{1,0:T(8,128)(2,1)} %get-tuple-element.9.refs_0_, bf16[768,128]{1,0:T(8,128)(2,1)} %get-tuple-element.10.refs_1_, f32[1536,128]{1,0:T(8,128)} %get-tuple-element.11.refs_2_), custom_call_target="tpu_custom_call" | custom-call | tf_op jit(solution)/shard_map/pallas_call | solution.py:713
